TPU v7x, 32 devices: a whole 2x2x4 slice. The times are simulated.
32 devices in a mesh: groups: 2 (over y), seq: 8 (over z, x), head: 1, sub: 2 (over core).
Axes of the slice: x: 2, y: 2, z: 4, core: 2. Of those that a mesh axis runs over, the one named last changes fastest.
Arguments:
- queries: bfloat16 [8, 32768, 512], P('head', ('groups', 'seq', 'sub')), parts along dimension 1, may hold values from -6 to 6
- keys: bfloat16 [8, 32768, 512], P('head', ('groups', 'seq', 'sub')), parts along dimension 1, may hold values from -6 to 6
- values: bfloat16 [8, 32768, 512], P('head', ('groups', 'seq', 'sub')), parts along dimension 1, may hold values from -6 to 6
- lr_codes: int32 [8, 32768], P('head', ('groups', 'seq', 'sub')), parts along dimension 1, may hold values from 0 to 15
- fast_gate: float32 [8, 512, 512], P('head', ('seq', 'sub')), may hold values from -0.25 to 0.25
- fast_up: float32 [8, 512, 512], P('head', ('seq', 'sub')), may hold values from -0.25 to 0.25
- fast_down: float32 [8, 512, 512], P('head', ('seq', 'sub')), may hold values from -0.25 to 0.25
Outputs:
- fast_out: bfloat16 [8, 32768, 512], P('head', ('groups', 'seq', 'sub')), parts along dimension 1
There are 2 independent parts, one for each index of `groups`. A program takes and returns all parts, laid end to end along the dimension named above; an argument that names none is the same for every part. Nothing has to cross between parts.
All inputs are finite; a program needn't handle non-finite values.
Results may differ from a plain program's by a relative error of at most 0.0085.
Values may be sent and summed in bfloat16 or wider, within the bound.
No kernel may reach another device: no remote copies, remote signals or barrier semaphores. Data moves between devices by JAX's collectives and lax.ppermute only.
A program may use at most 192 MiB of HBM per device.

v0:
```python
import jax
import jax.numpy as jnp
from jax import lax
from jax.sharding import PartitionSpec as P

EPSILON = 1e-06
STEP_SIZE = 0.5


def column_squares(matrix):
    return jnp.sum(matrix * matrix, axis=1)


def rescale(moved, col_weight, col_moved):
    return moved * jnp.sqrt((col_weight + EPSILON) / (col_moved + EPSILON))[:, None, :]


def step_scale(col_weight, grad_total):
    return (
        STEP_SIZE * jnp.sqrt(jnp.sum(col_weight, axis=1) + EPSILON) / jnp.sqrt(grad_total + EPSILON)
    )


def apply_fast(queries, gate_b, up_b, down_b):
    query_gate = jnp.einsum("htd,hdf->htf", queries, gate_b, preferred_element_type=jnp.float32)
    query_up = jnp.einsum("htd,hdf->htf", queries, up_b, preferred_element_type=jnp.float32)
    query_hidden = (jax.nn.silu(query_gate) * query_up).astype(jnp.bfloat16)
    return jnp.einsum(
        "htf,hfd->htd", query_hidden, down_b, preferred_element_type=jnp.float32
    ).astype(jnp.bfloat16)


def local_grads(keys, target, gate_b, up_b, down_b):
    gate_pre = jnp.einsum("htd,hdf->htf", keys, gate_b, preferred_element_type=jnp.float32)
    up_pre = jnp.einsum("htd,hdf->htf", keys, up_b, preferred_element_type=jnp.float32)
    sigmoid_gate = jax.nn.sigmoid(gate_pre)
    hidden = (gate_pre * sigmoid_gate * up_pre).astype(jnp.bfloat16)
    back = jnp.einsum("htd,hfd->htf", target, down_b, preferred_element_type=jnp.float32)
    grad_gate_pre = (back * up_pre * sigmoid_gate * (1.0 + gate_pre * (1.0 - sigmoid_gate))).astype(
        jnp.bfloat16
    )
    grad_up_pre = (back * gate_pre * sigmoid_gate).astype(jnp.bfloat16)
    grad_gate = jnp.einsum("htd,htf->hdf", keys, grad_gate_pre, preferred_element_type=jnp.float32)
    grad_up = jnp.einsum("htd,htf->hdf", keys, grad_up_pre, preferred_element_type=jnp.float32)
    grad_down = jnp.einsum("htf,htd->hfd", hidden, target, preferred_element_type=jnp.float32)
    return (grad_gate, grad_up, grad_down)


def on_device(queries, keys, values, lr_codes, fast_gate, fast_up, fast_down):
    token_rates = (lr_codes.astype(jnp.float32) + 1.0) / 16.0
    target = (-token_rates[:, :, None] * values.astype(jnp.float32)).astype(jnp.bfloat16)
    gate_b, up_b, down_b = (
        lax.all_gather(fast_gate.astype(jnp.bfloat16), ("seq", "sub"), axis=1, tiled=True),
        lax.all_gather(fast_up.astype(jnp.bfloat16), ("seq", "sub"), axis=1, tiled=True),
        lax.all_gather(fast_down.astype(jnp.bfloat16), ("seq", "sub"), axis=1, tiled=True),
    )
    grad_gate, grad_up, grad_down = local_grads(keys, target, gate_b, up_b, down_b)
    owned = (
        lax.psum_scatter(grad_gate, ("seq", "sub"), scatter_dimension=1, tiled=True),
        lax.psum_scatter(grad_up, ("seq", "sub"), scatter_dimension=1, tiled=True),
        lax.psum_scatter(grad_down, ("seq", "sub"), scatter_dimension=1, tiled=True),
    )
    weights = (fast_gate, fast_up, fast_down)
    grad_local = jnp.stack(
        [
            jnp.sum(owned[0] * owned[0], axis=(1, 2)),
            jnp.sum(owned[1] * owned[1], axis=(1, 2)),
            jnp.sum(owned[2] * owned[2], axis=(1, 2)),
        ],
        axis=1,
    )
    col_gate, col_up, col_down, grad_totals = lax.psum(
        (column_squares(fast_gate), column_squares(fast_up), column_squares(fast_down), grad_local),
        ("seq", "sub"),
    )
    col_weights = (col_gate, col_up, col_down)
    moved_all = []
    for index in range(3):
        scale = step_scale(col_weights[index], grad_totals[:, index])
        moved_all.append(weights[index] - scale[:, None, None] * owned[index])
    moved_cols = lax.psum(
        (column_squares(moved_all[0]), column_squares(moved_all[1]), column_squares(moved_all[2])),
        ("seq", "sub"),
    )
    renewed = [
        rescale(moved_all[index], col_weights[index], moved_cols[index]).astype(jnp.bfloat16)
        for index in range(3)
    ]
    new_gate, new_up, new_down = (
        lax.all_gather(renewed[0], ("seq", "sub"), axis=1, tiled=True),
        lax.all_gather(renewed[1], ("seq", "sub"), axis=1, tiled=True),
        lax.all_gather(renewed[2], ("seq", "sub"), axis=1, tiled=True),
    )
    return apply_fast(queries, new_gate, new_up, new_down)


def solution(mesh):
    return jax.shard_map(
        on_device,
        mesh=mesh,
        in_specs=(
            P("head", ("groups", "seq", "sub"), None),
            P("head", ("groups", "seq", "sub"), None),
            P("head", ("groups", "seq", "sub"), None),
            P("head", ("groups", "seq", "sub")),
            P("head", ("seq", "sub"), None),
            P("head", ("seq", "sub"), None),
            P("head", ("seq", "sub"), None),
        ),
        out_specs=P("head", ("groups", "seq", "sub"), None),
        check_vma=False,
    )
```

profile of v0, /device:TPU:0, one launch (start us, length us, event | category | flops | bytes accessed | tf_op | source)
XLA Modules:
  0.0 794.0 jit_solution(1773407533182401554)
XLA Ops:
  6.5 2.6 multiply_reduce_fusion.8
  9.2 2.6 multiply_reduce_fusion.1
  11.8 2.6 multiply_reduce_fusion.3
  15.3 47.5 %all-gather.11.cloned.1.call-done = bf16[8,512,512]{2,1,0:T(8,128)(2,1)} async-done(((bf16[8,32,512]{2,1,0:T(8,128)(2,1)}), bf16[8,512,512]{2,1,0:T(8,128)(2,1)}) %all-gather.11.cloned.1.call-update) | async-done | bytes 4194320 | tf_op jit(solution)/shard_map/all_gather | solution.py:53
  62.9 14.8 %fusion.19 = f32[8,1024,512]{2,1,0:T(8,128)} fusion(bf16[8,1024,512]{2,1,0:T(8,128)(2,1)} %param.8, bf16[8,512,512]{2,1,0:T(8,128)(2,1)} %all-gather.11.cloned.1.call-done), kind=kOutput, calls=%fused_computation.50 | convolution fusion | flops 4294967296 | bytes 29360128 | tf_op jit(solution)/shard_map/htd,hdf->htf/dot_general | solution.py:34
  77.7 36.5 %all-gather.7.cloned.1.call-done = bf16[8,512,512]{2,1,0:T(8,128)(2,1)} async-done(((bf16[8,32,512]{2,1,0:T(8,128)(2,1)}), bf16[8,512,512]{2,1,0:T(8,128)(2,1)}) %all-gather.7.cloned.1.call-update) | async-done | bytes 4194320 | tf_op jit(solution)/shard_map/all_gather | solution.py:55
  114.1 11.7 %fusion.7 = f32[8,1024,512]{2,1,0:T(8,128)} fusion(bf16[8,512,512]{2,1,0:T(8,128)(2,1)} %all-gather.7.cloned.1.call-done, bf16[8,1024,512]{2,1,0:T(8,128)(2,1)} %param.9, f32[8,1024]{1,0:T(8,128)S(1)} %multiply_negate_fusion), kind=kOutput, calls=%fused_computation.15 | convolution fusion | flops 4307550208 | bytes 29392896 | tf_op jit(solution)/shard_map/htd,hfd->htf/dot_general | solution.py:38
  125.8 19.5 %fusion.13 = f32[8,512,512]{1,2,0:T(8,128)} fusion(bf16[8,1024,512]{2,1,0:T(8,128)(2,1)} %param.8, f32[8,1024,512]{2,1,0:T(8,128)} %fusion.7, f32[8,1024,512]{2,1,0:T(8,128)} %fusion.19), kind=kOutput, calls=%fused_computation.21 | convolution fusion | flops 4320133120 | bytes 50331648 | tf_op jit(solution)/shard_map/htd,htf->hdf/dot_general | solution.py:44
  145.3 10.5 %copy.18 = f32[8,512,512]{2,0,1:T(8,128)} copy(f32[8,512,512]{1,2,0:T(8,128)} %fusion.13) | data formatting | bytes 16777216 | tf_op jit(solution)/shard_map/htd,htf->hdf/dot_general | solution.py:44
  156.0 9.4 %all-gather.9.cloned.1.call-done = bf16[8,512,512]{2,1,0:T(8,128)(2,1)} async-done(((bf16[8,32,512]{2,1,0:T(8,128)(2,1)}), bf16[8,512,512]{2,1,0:T(8,128)(2,1)}) %all-gather.9.cloned.1.call-update) | async-done | bytes 4194320 | tf_op jit(solution)/shard_map/all_gather | solution.py:54
  165.4 16.6 %fusion.18 = f32[8,1024,512]{2,1,0:T(8,128)} fusion(bf16[8,1024,512]{2,1,0:T(8,128)(2,1)} %param.8, bf16[8,512,512]{2,1,0:T(8,128)(2,1)} %all-gather.9.cloned.1.call-done), kind=kOutput, calls=%fused_computation.49 | convolution fusion | flops 4294967296 | bytes 29360128 | tf_op jit(solution)/shard_map/htd,hdf->htf/dot_general | solution.py:35
  182.0 21.8 %fusion.5 = f32[8,512,512]{2,1,0:T(8,128)} fusion(f32[8,1024,512]{2,1,0:T(8,128)} %fusion.18, f32[8,1024,512]{2,1,0:T(8,128)} %fusion.19, bf16[8,1024,512]{2,1,0:T(8,128)(2,1)} %param.9, f32[8,1024]{1,0:T(8,128)S(1)} %multiply_negate_fusion), kind=kOutput, calls=%fused_computation.13 | convolution fusion | flops 4332716032 | bytes 50364416 | tf_op jit(solution)/shard_map/htf,htd->hfd/dot_general | solution.py:45
  203.9 25.5 %fusion.12 = f32[8,512,512]{1,2,0:T(8,128)} fusion(bf16[8,1024,512]{2,1,0:T(8,128)(2,1)} %param.8, f32[8,1024,512]{2,1,0:T(8,128)} %fusion.19, f32[8,1024,512]{2,1,0:T(8,128)} %fusion.7, f32[8,1024,512]{2,1,0:T(8,128)} %fusion.18), kind=kOutput, calls=%fused_computation.20 | convolution fusion | flops 4336910336 | bytes 67108864 | tf_op jit(solution)/shard_map/htd,htf->hdf/dot_general | solution.py:43
  229.4 10.6 %copy.16 = f32[8,512,512]{2,0,1:T(8,128)} copy(f32[8,512,512]{1,2,0:T(8,128)} %fusion.12) | data formatting | bytes 16777216 | tf_op jit(solution)/shard_map/htd,htf->hdf/dot_general | solution.py:43
  240.1 32.5 %reduce-scatter.6.cloned.1.call-done = f32[8,32,512]{2,0,1:T(8,128)} async-done(((f32[8,512,512]{2,0,1:T(8,128)}), f32[8,32,512]{2,0,1:T(8,128)}) %reduce-scatter.6.cloned.1.call-update) | async-done | bytes 524304 | tf_op jit(solution)/shard_map/reduce_scatter | solution.py:60
  273.9 107.0 %reduce-scatter.8.cloned.1.call-done = f32[8,32,512]{2,1,0:T(8,128)} async-done(((f32[8,512,512]{2,1,0:T(8,128)}), f32[8,32,512]{2,1,0:T(8,128)}) %reduce-scatter.8.cloned.1.call-update) | async-done | bytes 524304 | tf_op jit(solution)/shard_map/reduce_scatter | solution.py:61
  382.2 107.2 %reduce-scatter.4.cloned.1.call-done = f32[8,32,512]{2,0,1:T(8,128)} async-done(((f32[8,512,512]{2,0,1:T(8,128)}), f32[8,32,512]{2,0,1:T(8,128)}) %reduce-scatter.4.cloned.1.call-update) | async-done | bytes 524304 | tf_op jit(solution)/shard_map/reduce_scatter | solution.py:59
  490.7 60.4 %all-reduce.1 = (f32[8,3]{0,1:T(4,128)S(1)}, f32[8,512]{1,0:T(8,128)S(1)}, f32[8,512]{1,0:T(8,128)S(1)}, f32[8,512]{1,0:T(8,128)S(1)}) all-reduce(f32[8,3]{0,1:T(4,128)S(1)} %pad_maximum_fusion, f32[8,512]{1,0:T(8,128)S(1)} %copy-done.5, ...), channel_id=1, replica_groups=mesh['groups'=2,'seq'=8,'head'=1,'sub'=2] {'seq','sub'}, use_global_device_ids=true, to_apply=%region_9.0 | all-reduce | flops 12312 | bytes 98496 | tf_op jit(solution)/shard_map/psum | solution.py:72
  554.6 57.7 %all-reduce = (f32[8,512]{1,0:T(8,128)S(1)}, f32[8,512]{1,0:T(8,128)S(1)}, f32[8,512]{1,0:T(8,128)S(1)}) all-reduce(f32[8,512]{1,0:T(8,128)S(1)} %multiply_reduce_fusion, f32[8,512]{1,0:T(8,128)S(1)} %get-tuple-element.22, f32[8,512]{1,0:T(8,128)S(1)} %get-tuple-element.21), channel_id=1, replica_groups=mesh['groups'=2,'seq'=8,'head'=1,'sub'=2] {'seq','sub'}, use_global_device_ids=true, to_apply=%region_21.0 | all-reduce | flops 12288 | bytes 98304 | tf_op jit(solution)/shard_map/psum | solution.py:81
  617.7 44.6 %all-gather.13.cloned.1.call-done = bf16[8,512,512]{2,0,1:T(8,128)(2,1)} async-done(((bf16[8,32,512]{2,0,1:T(8,128)(2,1)}), bf16[8,512,512]{2,0,1:T(8,128)(2,1)}) %all-gather.13.cloned.1.call-update) | async-done | bytes 4194320 | tf_op jit(solution)/shard_map/all_gather | solution.py:90
  662.3 14.9 %fusion.10 = f32[8,512,1024]{1,2,0:T(8,128)} fusion(bf16[8,1024,512]{2,1,0:T(8,128)(2,1)} %param.7, bf16[8,512,512]{2,0,1:T(8,128)(2,1)} %all-gather.13.cloned.1.call-done), kind=kOutput, calls=%fused_computation.18 | convolution fusion | flops 4294967296 | bytes 29360128 | tf_op jit(solution)/shard_map/htd,hdf->htf/dot_general | solution.py:25
  677.3 36.4 %all-gather.17.cloned.1.call-done = bf16[8,512,512]{2,1,0:T(8,128)(2,1)} async-done(((bf16[8,32,512]{2,1,0:T(8,128)(2,1)}), bf16[8,512,512]{2,1,0:T(8,128)(2,1)}) %all-gather.17.cloned.1.call-update) | async-done | bytes 4194320 | tf_op jit(solution)/shard_map/all_gather | solution.py:92
  713.6 51.2 %all-gather.15.cloned.1.call-done = bf16[8,512,512]{2,0,1:T(8,128)(2,1)} async-done(((bf16[8,32,512]{2,0,1:T(8,128)(2,1)}), bf16[8,512,512]{2,0,1:T(8,128)(2,1)}) %all-gather.15.cloned.1.call-update) | async-done | bytes 4194320 | tf_op jit(solution)/shard_map/all_gather | solution.py:91
  764.9 22.5 %convolution_convert_fusion = bf16[8,1024,512]{2,1,0:T(8,128)(2,1)} fusion(bf16[8,512,512]{2,1,0:T(8,128)(2,1)} %all-gather.17.cloned.1.call-done, f32[8,512,1024]{1,2,0:T(8,128)} %fusion.10, bf16[8,1024,512]{2,1,0:T(8,128)(2,1)} %param.7, bf16[8,512,512]{2,0,1:T(8,128)(2,1)} %all-gather.15.cloned.1.call-done), kind=kOutput, calls=%fused_computation.16 | convolution fusion | flops 8619294720 | bytes 41943040 | tf_op jit(solution)/shard_map/htf,hfd->htd/dot_general | solution.py:28
  (49 shorter events, 14.1 us)
Async XLA Ops:
  6.5 56.3 %all-gather.11.cloned.1.call-start = ((), (), s32[]{:S(2)}) async-start(), calls=%async_computation.5 | async-start | bytes 4456448 | tf_op jit(solution)/shard_map/all_gather | solution.py:53
  9.1 105.0 %all-gather.7.cloned.1.call-start = ((), (), s32[]{:S(2)}) async-start(), calls=%async_computation.3 | async-start | bytes 4456448 | tf_op jit(solution)/shard_map/all_gather | solution.py:55
  11.8 153.7 %all-gather.9.cloned.1.call-start = ((), (), s32[]{:S(2)}) async-start(), calls=%async_computation.4 | async-start | bytes 4456448 | tf_op jit(solution)/shard_map/all_gather | solution.py:54
  14.5 258.1 %reduce-scatter.6.cloned.1.call-start = ((), (), s32[]{:S(2)}) async-start(), calls=%async_computation.7 | async-start | bytes 8912896 | tf_op jit(solution)/shard_map/reduce_scatter | solution.py:60
  155.8 225.2 %reduce-scatter.8.cloned.1.call-start = ((), (), s32[]{:S(2)}) async-start(), calls=%async_computation.8 | async-start | bytes 8912896 | tf_op jit(solution)/shard_map/reduce_scatter | solution.py:61
  203.8 285.5 %reduce-scatter.4.cloned.1.call-start = ((), (), s32[]{:S(2)}) async-start(), calls=%async_computation.6 | async-start | bytes 8912896 | tf_op jit(solution)/shard_map/reduce_scatter | solution.py:59
  240.0 250.7 %copy-start.4 = (f32[8,512]{1,0:T(8,128)S(1)}, f32[8,512]{1,0:T(8,128)}, u32[]{:S(2)}) copy-start(f32[8,512]{1,0:T(8,128)} %get-tuple-element.14) | copy-start | bytes 49156
  240.0 250.7 %copy-start.5 = (f32[8,512]{1,0:T(8,128)S(1)}, f32[8,512]{1,0:T(8,128)}, u32[]{:S(2)}) copy-start(f32[8,512]{1,0:T(8,128)} %get-tuple-element.16) | copy-start | bytes 49156
  240.0 250.7 %copy-start.6 = (f32[8,512]{1,0:T(8,128)S(1)}, f32[8,512]{1,0:T(8,128)}, u32[]{:S(2)}) copy-start(f32[8,512]{1,0:T(8,128)} %get-tuple-element.12) | copy-start | bytes 49156
  240.0 311.4 %copy-start = (f32[8,32,512]{2,1,0:T(8,128)S(1)}, f32[8,32,512]{2,1,0:T(8,128)}, u32[]{:S(2)}) copy-start(f32[8,32,512]{2,1,0:T(8,128)} %param.13) | copy-start | bytes 1572868
  240.0 312.7 %copy-start.1 = (f32[8,32,512]{2,1,0:T(8,128)S(1)}, f32[8,32,512]{2,1,0:T(8,128)}, u32[]{:S(2)}) copy-start(f32[8,32,512]{2,1,0:T(8,128)} %param.11) | copy-start | bytes 1572868
  240.0 312.7 %copy-start.2 = (f32[8,32,512]{2,1,0:T(8,128)S(1)}, f32[8,32,512]{2,1,0:T(8,128)}, u32[]{:S(2)}) copy-start(f32[8,32,512]{2,1,0:T(8,128)} %param.12) | copy-start | bytes 1572868
  240.0 422.3 %all-gather.13.cloned.1.call-start = ((), (), s32[]{:S(2)}) async-start(), calls=%async_computation.9 | async-start | bytes 4456448 | tf_op jit(solution)/shard_map/all_gather | solution.py:90
  272.6 344.1 %copy-start.3 = (f32[8,32,512]{2,0,1:T(8,128)S(1)}, f32[8,32,512]{2,0,1:T(8,128)}, u32[]{:S(2)}) copy-start(f32[8,32,512]{2,0,1:T(8,128)} %reduce-scatter.6.cloned.1.call-done) | copy-start | bytes 1572868
  614.4 99.2 %all-gather.17.cloned.1.call-start = ((), (), s32[]{:S(2)}) async-start(), calls=%async_computation.11 | async-start | bytes 4456448 | tf_op jit(solution)/shard_map/all_gather | solution.py:92
  616.4 148.5 %all-gather.15.cloned.1.call-start = ((), (), s32[]{:S(2)}) async-start(), calls=%async_computation.10 | async-start | bytes 4456448 | tf_op jit(solution)/shard_map/all_gather | solution.py:91
Sparse Core Ops, SparseCore 0:
  9.5 53.2 all-gather.10
  65.0 49.0 all-gather.6
  116.3 49.0 all-gather.8
  169.4 103.1 reduce-scatter.5
  276.5 104.4 reduce-scatter.7
  384.9 104.4 reduce-scatter.3
  614.5 47.7 all-gather.12
  664.5 49.0 all-gather.16
  715.8 49.0 all-gather.14
where the time goes:
time: 795 us; the launch traced here: 794 us
  waiting for transfers between devices  472 us (59%)
  matrix products  147 us (18%)
  blocking collectives  118 us (15%)
  local copies, waits for them, and re-layouts  21.1 us (3%)
  other arithmetic  20.9 us (3%)
  between operations  13.3 us (2%)
    reduce_scatter x1, waiting for transfers between devices, on_device(): lax.psum_scatter(grad_gate, ('seq', 'sub'), scatter_dimension=1, tiled=True)  107 us
    reduce_scatter x1, waiting for transfers between devices, on_device(): lax.psum_scatter(grad_down, ('seq', 'sub'), scatter_dimension=1, tiled=True)  107 us
    psum x1, blocking collectives, on_device(): lax.psum((column_squares(fast_gate), column_squares(fast_up), column_squa...  60.4 us
    psum x1, blocking collectives, on_device(): lax.psum((column_squares(moved_all[0]), column_squares(moved_all[1]), col...  57.7 us
    all_gather x1, waiting for transfers between devices, on_device(): lax.all_gather(renewed[1], ('seq', 'sub'), axis=1, tiled=True)  51.2 us
    all_gather x1, waiting for transfers between devices, on_device(): lax.all_gather(fast_gate.astype(jnp.bfloat16), ('seq', 'sub'), axis=1, ti...  47.5 us
    all_gather x1, waiting for transfers between devices, on_device(): lax.all_gather(renewed[0], ('seq', 'sub'), axis=1, tiled=True)  44.6 us
    all_gather x1, waiting for transfers between devices, on_device(): lax.all_gather(fast_down.astype(jnp.bfloat16), ('seq', 'sub'), axis=1, ti...  36.5 us
  transfers between devices with their start and end apart: 9, of which 9 were waited for; matrix products, arithmetic and copies ran while one was open for 20% of the time, Pallas kernels for 0%

commit v1 on v0

--- a/solution.py
+++ b/solution.py
@@ -1,10 +1,17 @@
+import functools
+
 import jax
 import jax.numpy as jnp
 from jax import lax
+from jax.experimental import pallas as pl
+from jax.experimental.pallas import tpu as pltpu
 from jax.sharding import PartitionSpec as P
 
 EPSILON = 1e-06
 STEP_SIZE = 0.5
+BF16 = jnp.bfloat16
+F32 = jnp.float32
+VMEM_LIMIT = 56 * 1024 * 1024
 
 
 def column_squares(matrix):
@@ -46,7 +53,7 @@
     return (grad_gate, grad_up, grad_down)
 
 
-def on_device(queries, keys, values, lr_codes, fast_gate, fast_up, fast_down):
+def on_device_generic(queries, keys, values, lr_codes, fast_gate, fast_up, fast_down):
     token_rates = (lr_codes.astype(jnp.float32) + 1.0) / 16.0
     target = (-token_rates[:, :, None] * values.astype(jnp.float32)).astype(jnp.bfloat16)
     gate_b, up_b, down_b = (
@@ -94,7 +101,325 @@
     return apply_fast(queries, new_gate, new_up, new_down)
 
 
+def block(shape, index_map):
+    return pl.BlockSpec(shape, index_map)
+
+
+def whole(array):
+    return pl.BlockSpec(array.shape, lambda *_: (0,) * array.ndim)
+
+
+def anywhere():
+    return pl.BlockSpec(memory_space=pl.ANY)
+
+
+def call(body, name, positions, grid, operands, in_specs, out_shapes, out_specs, scratch=(), aliases=None, cost=None):
+    return pl.pallas_call(
+        body,
+        name=name,
+        out_shape=out_shapes,
+        grid_spec=pltpu.PrefetchScalarGridSpec(
+            num_scalar_prefetch=1,
+            grid=grid,
+            in_specs=in_specs,
+            out_specs=out_specs,
+            scratch_shapes=list(scratch),
+        ),
+        input_output_aliases=aliases or {},
+        compiler_params=pltpu.CompilerParams(vmem_limit_bytes=VMEM_LIMIT),
+        cost_estimate=cost,
+    )(positions, *operands)
+
+
+def sds(shape, dtype):
+    return jax.ShapeDtypeStruct(shape, dtype)
+
+
+def rounded_rows(positions, weights, half):
+    _, rows, columns = weights[0].shape
+
+    def body(pos, *refs):
+        for i in range(3):
+            refs[6][0, i] = refs[i][0].astype(BF16)
+            refs[7][0, i] = refs[3 + i][0].astype(BF16)
+
+    mine = block((1, rows, columns), lambda s, pos: (pos[0] * half + s, 0, 0))
+    other = block((1, rows, columns), lambda s, pos: ((1 - pos[0]) * half + s, 0, 0))
+    out = block((1, 3, rows, columns), lambda s, pos: (s, 0, 0, 0))
+    shape = sds((half, 3, rows, columns), BF16)
+    return call(body, "rounded_rows", positions, (half,), (*weights, *weights), [mine] * 3 + [other] * 3, [shape] * 2, [out] * 2)
+
+
+def first_piece(positions, own, received, stage, after):
+    _, _, rows, columns = own.shape
+    width = columns // 2
+
+    def body(pos, own_ref, received_ref, *rest):
+        out_ref = rest[-1]
+        mine = pl.ds(pl.multiple_of(pos[0] * rows, rows), rows)
+        theirs = pl.ds(pl.multiple_of((1 - pos[0]) * rows, rows), rows)
+        out_ref[:, mine, :] = own_ref[0]
+        out_ref[:, theirs, :] = received_ref[0]
+
+    spec = block((1, 3, rows, width), lambda i, pos: (stage, 0, 0, pos[3]))
+    shape = sds((3, 2 * rows, width), BF16)
+    return call(body, "first_piece", positions, (1,), (own, received, *after), [spec, spec] + [anywhere()] * len(after), shape, whole(shape))
+
+
+def gradients(positions, keys, keys_in, target, target_in, pieces, stage, half, tile):
+    z_size, _, piece_rows, width = pieces[0].shape
+    rows, columns = z_size * 2 * piece_rows, 2 * width
+    quarter = rows // z_size
+    tokens = keys.shape[1]
+    steps = tokens // tile
+
+    def body(pos, k0, k1, t0, t1, p0, p1, p2, p3, keep, send, own_w, squares, w, total):
+        step = pl.program_id(0)
+        z, x, y = pos[1], pos[2], pos[3]
+        mine = pl.ds(pl.multiple_of(x * width, 128), width)
+        theirs = pl.ds(pl.multiple_of((1 - x) * width, 128), width)
+
+        @pl.when(step == 0)
+        def _():
+            for i, (ref, xx, yy) in enumerate(((p0, x, y), (p1, 1 - x, y), (p2, x, 1 - y), (p3, 1 - x, 1 - y))):
+                cols = pl.ds(pl.multiple_of(yy * width, 128), width)
+                for j in range(z_size):
+                    at = pl.ds(pl.multiple_of((z ^ j) * quarter + xx * piece_rows, piece_rows), piece_rows)
+                    w[:, at, cols] = ref[j]
+            own_w[...] = w[:, pl.ds(pl.multiple_of(z * quarter, quarter), quarter), mine]
+            for m in range(3):
+                full = w[m].astype(F32)
+                squares[m : m + 1, :] = jnp.sum(full * full, axis=0, keepdims=True)
+
+        for n, (k_ref, t_ref) in enumerate(((k0, t0), (k1, t1))):
+            k, t = k_ref[0], t_ref[0]
+            gate = jnp.dot(k, w[0], preferred_element_type=F32)
+            up = jnp.dot(k, w[1], preferred_element_type=F32)
+            back = lax.dot_general(t, w[2], (((1,), (1,)), ((), ())), preferred_element_type=F32)
+            sig = 0.5 * jnp.tanh(0.5 * gate) + 0.5
+            silu = gate * sig
+            hidden = (silu * up).astype(BF16)
+            grad_up = (back * silu).astype(BF16)
+            grad_gate = (back * up * (sig + silu * (1.0 - sig))).astype(BF16)
+            for m, (a, b) in enumerate(((k, grad_gate), (k, grad_up), (hidden, t))):
+                part = lax.dot_general(a, b, (((0,), (0,)), ((), ())), preferred_element_type=F32)
+                if n == 0:
+                    @pl.when(step == 0)
+                    def _(m=m, part=part):
+                        total[m] = part
+
+                    @pl.when(step > 0)
+                    def _(m=m, part=part):
+                        total[m] += part
+                else:
+                    total[m] += part
+
+        @pl.when(step == steps - 1)
+        def _():
+            keep[...] = total[:, :, mine]
+            send[...] = total[:, :, theirs].astype(BF16)
+
+    here = block((1, tile, columns), lambda i, pos: (pos[0] * half + stage, i, 0))
+    there = block((1, tile, columns), lambda i, pos: (stage, i, 0))
+    outs = [sds((3, rows, width), F32), sds((3, rows, width), BF16), sds((3, quarter, width), BF16), sds((8, columns), F32)]
+    flops = 6 * 2 * 2 * tokens * rows * columns
+    return call(
+        body, "gradients", positions, (steps,),
+        (keys, keys_in, target, target_in, *pieces),
+        [here, there, here, there] + [whole(p) for p in pieces],
+        outs, [whole(o) for o in outs],
+        [pltpu.VMEM((3, rows, columns), BF16), pltpu.VMEM((3, rows, columns), F32)],
+        cost=pl.CostEstimate(flops=flops, bytes_accessed=14 * 2**20, transcendentals=2 * tokens * columns),
+    )
+
+
+def add_halves(positions, keep, received, z_size):
+    _, rows, width = keep.shape
+    quarter = rows // z_size
+
+    def body(pos, keep_ref, received_ref, own, *sends):
+        for j in range(z_size):
+            at = pl.ds(pl.multiple_of((pos[1] ^ j) * quarter, quarter), quarter)
+            added = keep_ref[:, at, :] + received_ref[:, at, :].astype(F32)
+            if j == 0:
+                own[...] = added
+            else:
+                sends[j - 1][...] = added.astype(BF16)
+
+    outs = [sds((3, quarter, width), F32)] + [sds((3, quarter, width), BF16)] * (z_size - 1)
+    return call(body, "add_halves", positions, (1,), (keep, received), [whole(keep), whole(received)], outs, [whole(o) for o in outs])
+
+
+def column_sums(positions, own, received, own_w):
+    def body(pos, own_ref, *refs):
+        parts, w_ref, grad, sums = refs[:-3], refs[-3], refs[-2], refs[-1]
+        sums[...] = jnp.zeros_like(sums)
+        for m in range(3):
+            g = own_ref[m]
+            for part in parts:
+                g = g + part[m].astype(F32)
+            grad[m] = g
+            sums[m : m + 1, :] = jnp.sum(g * g, axis=0, keepdims=True)
+            sums[3 + m : 4 + m, :] = jnp.sum(g * w_ref[m].astype(F32), axis=0, keepdims=True)
+
+    outs = [sds(own.shape, F32), sds((8, own.shape[2]), F32)]
+    operands = (own, *received, own_w)
+    return call(body, "column_sums", positions, (1,), operands, [whole(a) for a in operands], outs, [whole(o) for o in outs])
+
+
+def renewed_block(positions, grad, own_w, squares, sums, others):
+    width = grad.shape[2]
+
+    def body(pos, g_ref, w_ref, sq_ref, sums_ref, *refs):
+        out = refs[-1]
+        here = sums_ref[...]
+        there = jnp.zeros_like(here)
+        for i, ref in enumerate(refs[:-1]):
+            if i % 2:
+                here = here + ref[...]
+            else:
+                there = there + ref[...]
+        mine = pl.ds(pl.multiple_of(pos[2] * width, 128), width)
+        for m in range(3):
+            total_g = jnp.sum(here[m : m + 1] + there[m : m + 1], axis=1, keepdims=True)
+            total_w = jnp.sum(sq_ref[m : m + 1, :], axis=1, keepdims=True)
+            scale = STEP_SIZE * jnp.sqrt(total_w + EPSILON) / jnp.sqrt(total_g + EPSILON)
+            col_w = sq_ref[m : m + 1, mine]
+            col_moved = col_w - 2.0 * scale * here[3 + m : 4 + m] + scale * scale * here[m : m + 1]
+            ratio = jnp.sqrt((col_w + EPSILON) / (jnp.maximum(col_moved, 0.0) + EPSILON))
+            out[m] = ((w_ref[m].astype(F32) - scale * g_ref[m]) * ratio).astype(BF16)
+
+    operands = (grad, own_w, squares, sums, *others)
+    shape = sds(grad.shape, BF16)
+    return call(body, "renewed_block", positions, (1,), operands, [whole(a) for a in operands], shape, whole(shape))
+
+
+def apply_renewed(positions, queries, queries_in, held, swapped, stage, half, tile, out, late):
+    z_size, _, quarter, width = held.shape
+    rows, columns = z_size * quarter, 2 * width
+    heads, tokens, _ = queries.shape
+    steps = tokens // tile
+    n_late = 0 if late is None else 1
+    n_out = 0 if out is None else 1
+
+    def body(pos, q0, q1, h_ref, s_ref, *refs):
+        w = refs[-1]
+        send_ref, out_refs = refs[-2], refs[n_late + n_out : -2]
+        z, x = pos[1], pos[2]
+
+        @pl.when(pl.program_id(0) == 0)
+        def _():
+            for ref, xx in ((h_ref, x), (s_ref, 1 - x)):
+                cols = pl.ds(pl.multiple_of(xx * width, 128), width)
+                for j in range(z_size):
+                    at = pl.ds(pl.multiple_of((z ^ j) * quarter, quarter), quarter)
+                    w[:, at, cols] = ref[j]
+
+        for q_ref, is_own in ((q0, True), (q1, False)):
+            q = q_ref[0]
+            gate = jnp.dot(q, w[0], preferred_element_type=F32)
+            up = jnp.dot(q, w[1], preferred_element_type=F32)
+            hidden = (gate * (0.5 * jnp.tanh(0.5 * gate) + 0.5) * up).astype(BF16)
+            result = jnp.dot(hidden, w[2], preferred_element_type=F32).astype(BF16)
+            if is_own:
+                out_refs[0][0] = result
+            else:
+                send_ref[...] = result
+
+    mine = lambda i, pos: (pos[0] * half + stage, i, 0)
+    here = block((1, tile, columns), mine)
+    there = block((1, tile, columns), lambda i, pos: (stage, i, 0))
+    operands = [queries, queries_in, held, swapped]
+    in_specs = [here, there, whole(held), whole(swapped)]
+    aliases = {}
+    if out is not None:
+        aliases = {1 + len(operands): 0}
+        operands.append(out)
+        in_specs.append(anywhere())
+    return call(
+        body, "apply_renewed", positions, (steps,), operands, in_specs,
+        [sds(queries.shape, BF16), sds((tokens, columns), BF16)],
+        [block((1, tile, columns), mine), block((tile, columns), lambda i, pos: (i, 0))],
+        [pltpu.VMEM((3, rows, columns), BF16)],
+        aliases,
+        pl.CostEstimate(flops=3 * 2 * 2 * tokens * rows * columns, bytes_accessed=7 * 2**20, transcendentals=2 * tokens * columns),
+    )
+
+
+def place(positions, out, received, stage, half):
+    def body(pos, received_ref, _, out_ref):
+        out_ref[0] = received_ref[...]
+
+    tokens, columns = received.shape
+    spec = block((1, tokens, columns), lambda i, pos: ((1 - pos[0]) * half + stage, 0, 0))
+    return call(body, "place", positions, (1,), (received, out), [whole(received), anywhere()], sds(out.shape, BF16), spec, aliases={2: 0})
+
+
+def on_device_fast(z_size, queries, keys, values, lr_codes, fast_gate, fast_up, fast_down):
+    heads, tokens, _ = queries.shape
+    half = heads // 2
+    seq_size = 2 * z_size
+    core, seq = lax.axis_index("sub"), lax.axis_index("seq")
+    positions = jnp.stack([core, seq // 2, seq % 2, lax.axis_index("groups")]).astype(jnp.int32)
+    flip = [(0, 1), (1, 0)]
+    tile = 512 if tokens % 512 == 0 else tokens
+
+    def over_sub(a):
+        return lax.ppermute(a, "sub", flip)
+
+    def over_groups(a):
+        return lax.ppermute(a, "groups", flip)
+
+    def over_seq(a, bits):
+        return lax.ppermute(a, "seq", [(i, i ^ bits) for i in range(seq_size)])
+
+    def other_half(a):
+        return lax.dynamic_slice_in_dim(a, (1 - core) * half, half, axis=0)
+
+    own_rows, sent_rows = rounded_rows(positions, (fast_gate, fast_up, fast_down), half)
+    received_rows = over_sub(sent_rows)
+    token_rates = (lr_codes.astype(F32) + 1.0) / 16.0
+    target = (-token_rates[:, :, None] * values.astype(F32)).astype(BF16)
+    keys_in, target_in, queries_in = (over_sub(other_half(a)) for a in (keys, target, queries))
+
+    pieces, after = [], ()
+    for stage in range(half):
+        piece = first_piece(positions, own_rows, received_rows, stage, after)
+        after = tuple(over_seq(piece, 2 * j) for j in range(1, z_size))
+        held = jnp.stack((piece, *after))
+        swapped = over_seq(held, 1)
+        pieces.append((held, swapped, over_groups(held), over_groups(swapped)))
+
+    out, late = None, None
+    for stage in range(half):
+        keep, send, own_w, squares = gradients(
+            positions, keys, keys_in, target, target_in, pieces[stage], stage, half, tile
+        )
+        own, *sends = add_halves(positions, keep, over_seq(send, 1), z_size)
+        received = [over_seq(a, 2 * (j + 1)) for j, a in enumerate(sends)]
+        grad, sums = column_sums(positions, own, received, own_w)
+        others = [over_seq(sums, bits) for bits in range(1, seq_size)]
+        renewed = renewed_block(positions, grad, own_w, squares, sums, others)
+        held = jnp.stack([renewed] + [over_seq(renewed, 2 * j) for j in range(1, z_size)])
+        out, sent = apply_renewed(
+            positions, queries, queries_in, held, over_seq(held, 1), stage, half, tile, out, None
+        )
+        late = late or []
+        late.append(over_sub(sent))
+    for stage in range(half):
+        out = place(positions, out, late[stage], stage, half)
+    return out
+
+
 def solution(mesh):
+    seq, sub, groups = mesh.shape["seq"], mesh.shape["sub"], mesh.shape["groups"]
+
+    def on_device(queries, *rest):
+        fits = sub == 2 and groups == 2 and seq in (4, 8, 16) and queries.shape[0] % 2 == 0 and rest[3].shape[1] * seq * sub == 512
+        if fits:
+            return on_device_fast(seq // 2, queries, *rest)
+        return on_device_generic(queries, *rest)
+
     return jax.shard_map(
         on_device,
         mesh=mesh,

time: 795 us -> 475 us (0.60)
  waiting for transfers between devices: 472 us -> 170 us
  matrix products: 147 us -> 0 us
  Pallas kernels: 0 us -> 146 us
  blocking collectives: 118 us -> 0 us
  starting transfers between devices: 0.74 us -> 113 us
  between operations: 13.3 us -> 1.15 us
  other arithmetic: 20.9 us -> 8.76 us
  local copies, waits for them, and re-layouts: 21.1 us -> 29.8 us
    reduce_scatter x3 -> x0, waiting for transfers between devices: 247 us -> none  [the longest x1 107 us: on_device(): lax.psum_scatter(grad_gate, ('seq', 'sub'), scatter_dimension=1, tiled=True)]
    all_gather x6 -> x0, waiting for transfers between devices: 226 us -> none  [the longest x1 51.2 us: on_device(): lax.all_gather(renewed[1], ('seq', 'sub'), axis=1, tiled=True)]
    ppermute x0 -> x92, waiting for transfers between devices: none -> 170 us  [the longest x76 150 us: over_seq(): return lax.ppermute(a, 'seq', [(i, i ^ bits) for i in range(seq_size)])]
    dot_general x8 -> x0, matrix products: 147 us -> none  [the longest x1 25.5 us: local_grads(): jnp.einsum('htd,htf->hdf', keys, grad_gate_pre, preferred_element_type=jn...]
    pallas_call x0 -> x29, Pallas kernels: none -> 146 us  [call(): pl.pallas_call(body, name=name, out_shape=out_shapes, grid_spec=pltpu.Pre...]
    psum x2 -> x0, blocking collectives: 118 us -> none  [the longest x1 60.4 us: on_device(): lax.psum((column_squares(fast_gate), column_squares(fast_up), column_squa...]
    ppermute x0 -> x92, starting transfers between devices: none -> 113 us  [the longest x76 101 us: over_seq(): return lax.ppermute(a, 'seq', [(i, i ^ bits) for i in range(seq_size)])]
    dot_general x2 -> x0, local copies, waits for them, and re-layouts: 21.1 us -> none  [the longest x1 10.6 us: local_grads(): jnp.einsum('htd,htf->hdf', keys, grad_gate_pre, preferred_element_type=jn...]
  transfers between devices with their start and end apart: 9 -> 92, of which waited for: 9 -> 37; matrix products, arithmetic and copies ran while one was open for 20% -> 3% of each run, Pallas kernels for 0% -> 31%
where the time goes in v1:
time: 475 us; the launch traced here: 468 us
  waiting for transfers between devices  170 us (36%)
  Pallas kernels  146 us (31%)
  starting transfers between devices  113 us (24%)
  local copies, waits for them, and re-layouts  29.8 us (6%)
  other arithmetic  8.76 us (2%)
    ppermute x76, waiting for transfers between devices, over_seq(): return lax.ppermute(a, 'seq', [(i, i ^ bits) for i in range(seq_size)])  150 us
    pallas_call x29, Pallas kernels, call(): pl.pallas_call(body, name=name, out_shape=out_shapes, grid_spec=pltpu.Pre...  146 us
    ppermute x76, starting transfers between devices, over_seq(): return lax.ppermute(a, 'seq', [(i, i ^ bits) for i in range(seq_size)])  101 us
    unnamed x180, local copies, waits for them, and re-layouts  18.3 us
    ppermute x8, waiting for transfers between devices, over_groups(): return lax.ppermute(a, 'groups', flip)  16.4 us
    dynamic_slice x3, local copies, waits for them, and re-layouts, other_half(): return lax.dynamic_slice_in_dim(a, (1 - core) * half, half, axis=0)  11.5 us
  transfers between devices with their start and end apart: 92, of which 37 were waited for; matrix products, arithmetic and copies ran while one was open for 3% of the time, Pallas kernels for 31%

profile of v1, /device:TPU:0, one launch (start us, length us, event | category | flops | bytes accessed | tf_op | source)
XLA Modules:
  0.0 467.6 jit_solution(8829714137229043349)
XLA Ops:
  0.0 4.8 %constant_dynamic-slice_fusion.1 = bf16[4,1024,512]{2,1,0:T(8,128)(2,1)} fusion(bf16[8,1024,512]{2,1,0:T(8,128)(2,1)} %k0.7, s32[]{:T(128)S(6)} %select_n.18), kind=kLoop, calls=%fused_computation.11 | loop fusion | bytes 8388612 | tf_op jit(solution)/shard_map/dynamic_slice | solution.py:377
  31.0 7.5 %collective-permute-done.5.rest_1_ = bf16[3,64,256]{2,1,0:T(8,128)(2,1)S(1)} collective-permute-done((bf16[3,64,256]{2,1,0:T(8,128)(2,1)}, bf16[3,64,256]{2,1,0:T(8,128)(2,1)S(1)}, u32[]{:S(2)}, u32[]{:S(2)}) %collective-permute-start.5) | collective-permute-done | bytes 98336 | tf_op jit(solution)/shard_map/ppermute | solution.py:374
  47.3 5.5 %collective-permute-done.8.rest_1_ = bf16[3,64,256]{2,1,0:T(8,128)(2,1)S(1)} collective-permute-done((bf16[3,64,256]{2,1,0:T(8,128)(2,1)}, bf16[3,64,256]{2,1,0:T(8,128)(2,1)S(1)}, u32[]{:S(2)}, u32[]{:S(2)}) %collective-permute-start.8) | collective-permute-done | bytes 98336 | tf_op jit(solution)/shard_map/ppermute | solution.py:374
  61.5 5.8 %collective-permute-done.11.rest_1_ = bf16[3,64,256]{2,1,0:T(8,128)(2,1)S(1)} collective-permute-done((bf16[3,64,256]{2,1,0:T(8,128)(2,1)}, bf16[3,64,256]{2,1,0:T(8,128)(2,1)S(1)}, u32[]{:S(2)}, u32[]{:S(2)}) %collective-permute-start.11) | collective-permute-done | bytes 98336 | tf_op jit(solution)/shard_map/ppermute | solution.py:374
  86.6 7.3 %collective-permute-done.16.p1 = bf16[4,3,64,256]{3,2,1,0:T(8,128)(2,1)S(1)} collective-permute-done((bf16[4,3,64,256]{3,2,1,0:T(8,128)(2,1)S(1)}, bf16[4,3,64,256]{3,2,1,0:T(8,128)(2,1)S(1)}, u32[]{:S(2)}, u32[]{:S(2)}) %collective-permute-start.16) | collective-permute-done | bytes 393248 | tf_op jit(solution)/shard_map/ppermute | solution.py:374
  95.5 4.5 constant_dynamic-slice_fusion.2
  105.3 14.2 %gradients.4 = (f32[3,512,256]{2,1,0:T(8,128)}, bf16[3,512,256]{2,1,0:T(8,128)(2,1)}, bf16[3,128,256]{2,1,0:T(8,128)(2,1)}, f32[8,512]{1,0:T(8,128)}) custom-call(s32[4]{0:T(128)} %pad_add_fusion.pos, bf16[8,1024,512]{2,1,0:T(8,128)(2,1)} %k0.7, bf16[4,1024,512]{2,1,0:T(8,128)(2,1)} %collective-permute-done.1.k1, bf16[8,1024,512]{2,1,0:T(8,128)(2,1)} %copy-done, ...), custom_call_target="tpu_custom_call" | custom-call | flops 6442450944 | bytes 14680064 | tf_op jit(solution)/shard_map/gradients/pallas_call | solution.py:117
  123.7 14.3 %gradients.5 = (f32[3,512,256]{2,1,0:T(8,128)}, bf16[3,512,256]{2,1,0:T(8,128)(2,1)}, bf16[3,128,256]{2,1,0:T(8,128)(2,1)}, f32[8,512]{1,0:T(8,128)}) custom-call(s32[4]{0:T(128)} %pad_add_fusion.pos, bf16[8,1024,512]{2,1,0:T(8,128)(2,1)} %k0.7, bf16[4,1024,512]{2,1,0:T(8,128)(2,1)} %collective-permute-done.1.k1, bf16[8,1024,512]{2,1,0:T(8,128)(2,1)} %copy-done, ...), custom_call_target="tpu_custom_call" | custom-call | flops 6442450944 | bytes 14680064 | tf_op jit(solution)/shard_map/gradients/pallas_call | solution.py:117
  141.0 14.4 %collective-permute-done.54.p3 = bf16[4,3,64,256]{3,2,1,0:T(8,128)(2,1)S(1)} collective-permute-done((bf16[4,3,64,256]{3,2,1,0:T(8,128)(2,1)S(1)}, bf16[4,3,64,256]{3,2,1,0:T(8,128)(2,1)S(1)}, u32[]{:S(2)}, u32[]{:S(2)}) %collective-permute-start.54) | collective-permute-done | bytes 393248 | tf_op jit(solution)/shard_map/ppermute | solution.py:371
  156.9 14.2 %gradients.6 = (f32[3,512,256]{2,1,0:T(8,128)}, bf16[3,512,256]{2,1,0:T(8,128)(2,1)}, bf16[3,128,256]{2,1,0:T(8,128)(2,1)}, f32[8,512]{1,0:T(8,128)}) custom-call(s32[4]{0:T(128)} %pad_add_fusion.pos, bf16[8,1024,512]{2,1,0:T(8,128)(2,1)} %k0.7, bf16[4,1024,512]{2,1,0:T(8,128)(2,1)} %collective-permute-done.1.k1, bf16[8,1024,512]{2,1,0:T(8,128)(2,1)} %copy-done, ...), custom_call_target="tpu_custom_call" | custom-call | flops 6442450944 | bytes 14680064 | tf_op jit(solution)/shard_map/gradients/pallas_call | solution.py:117
  171.9 14.4 %gradients.7 = (f32[3,512,256]{2,1,0:T(8,128)}, bf16[3,512,256]{2,1,0:T(8,128)(2,1)}, bf16[3,128,256]{2,1,0:T(8,128)(2,1)}, f32[8,512]{1,0:T(8,128)}) custom-call(s32[4]{0:T(128)} %pad_add_fusion.pos, bf16[8,1024,512]{2,1,0:T(8,128)(2,1)} %k0.7, bf16[4,1024,512]{2,1,0:T(8,128)(2,1)} %collective-permute-done.1.k1, bf16[8,1024,512]{2,1,0:T(8,128)(2,1)} %copy-done, ...), custom_call_target="tpu_custom_call" | custom-call | flops 6442450944 | bytes 14680064 | tf_op jit(solution)/shard_map/gradients/pallas_call | solution.py:117
  199.6 8.1 %collective-permute-done.73.received_ref = bf16[3,512,256]{2,1,0:T(8,128)(2,1)S(1)} collective-permute-done((bf16[3,512,256]{2,1,0:T(8,128)(2,1)}, bf16[3,512,256]{2,1,0:T(8,128)(2,1)S(1)}, u32[]{:S(2)}, u32[]{:S(2)}) %collective-permute-start.73) | collective-permute-done | bytes 786464 | tf_op jit(solution)/shard_map/ppermute | solution.py:374
  220.9 13.2 %collective-permute-done.39.refs_1_ = bf16[3,128,256]{2,1,0:T(8,128)(2,1)S(1)} collective-permute-done((bf16[3,128,256]{2,1,0:T(8,128)(2,1)}, bf16[3,128,256]{2,1,0:T(8,128)(2,1)S(1)}, u32[]{:S(2)}, u32[]{:S(2)}) %collective-permute-start.39) | collective-permute-done | bytes 196640 | tf_op jit(solution)/shard_map/ppermute | solution.py:374
  247.9 13.5 %collective-permute-done.57.refs_1_ = bf16[3,128,256]{2,1,0:T(8,128)(2,1)S(1)} collective-permute-done((bf16[3,128,256]{2,1,0:T(8,128)(2,1)}, bf16[3,128,256]{2,1,0:T(8,128)(2,1)S(1)}, u32[]{:S(2)}, u32[]{:S(2)}) %collective-permute-start.57) | collective-permute-done | bytes 196640 | tf_op jit(solution)/shard_map/ppermute | solution.py:374
  288.6 8.6 %collective-permute-done.28.refs_5_ = f32[8,256]{1,0:T(8,128)S(1)} collective-permute-done((f32[8,256]{1,0:T(8,128)}, f32[8,256]{1,0:T(8,128)S(1)}, u32[]{:S(2)}, u32[]{:S(2)}) %collective-permute-start.28) | collective-permute-done | bytes 8224 | tf_op jit(solution)/shard_map/ppermute | solution.py:374
  351.6 4.7 %collective-permute-done.62.refs_3_ = f32[8,256]{1,0:T(8,128)S(1)} collective-permute-done((f32[8,256]{1,0:T(8,128)}, f32[8,256]{1,0:T(8,128)S(1)}, u32[]{:S(2)}, u32[]{:S(2)}) %collective-permute-start.62) | collective-permute-done | bytes 8224 | tf_op jit(solution)/shard_map/ppermute | solution.py:374
  357.0 7.3 %collective-permute-done.63.refs_4_ = f32[8,256]{1,0:T(8,128)S(1)} collective-permute-done((f32[8,256]{1,0:T(8,128)}, f32[8,256]{1,0:T(8,128)S(1)}, u32[]{:S(2)}, u32[]{:S(2)}) %collective-permute-start.63) | collective-permute-done | bytes 8224 | tf_op jit(solution)/shard_map/ppermute | solution.py:374
  364.2 5.9 %collective-permute-done.64.refs_5_ = f32[8,256]{1,0:T(8,128)S(1)} collective-permute-done((f32[8,256]{1,0:T(8,128)}, f32[8,256]{1,0:T(8,128)S(1)}, u32[]{:S(2)}, u32[]{:S(2)}) %collective-permute-start.64) | collective-permute-done | bytes 8224 | tf_op jit(solution)/shard_map/ppermute | solution.py:374
  392.5 7.5 %collective-permute-done.67 = bf16[3,128,256]{2,1,0:T(8,128)(2,1)S(1)} collective-permute-done((bf16[3,128,256]{2,1,0:T(8,128)(2,1)}, bf16[3,128,256]{2,1,0:T(8,128)(2,1)S(1)}, u32[]{:S(2)}, u32[]{:S(2)}) %collective-permute-start.67) | collective-permute-done | bytes 196640 | tf_op jit(solution)/shard_map/ppermute | solution.py:374
  411.5 4.5 collective-permute-done.31
  421.1 7.3 %apply_renewed.4 = (bf16[8,1024,512]{2,1,0:T(8,128)(2,1)}, bf16[1024,512]{1,0:T(8,128)(2,1)}) custom-call(s32[4]{0:T(128)} %pad_add_fusion.pos, bf16[8,1024,512]{2,1,0:T(8,128)(2,1)} %q0.7, bf16[4,1024,512]{2,1,0:T(8,128)(2,1)} %copy-done.1, bf16[4,3,128,256]{3,2,1,0:T(8,128)(2,1)} %copy-done.7, bf16[4,3,128,256]{3,2,1,0:T(8,128)(2,1)} %collective-permute-done.87.s_ref), custom_call_target="tpu_custom_call" | custom-call | flops 3221225472 | bytes 7340032 | tf_op jit(solution)/shard_map/apply_renewed/pallas_call | solution.py:117
  429.3 7.0 %apply_renewed.5 = (bf16[8,1024,512]{2,1,0:T(8,128)(2,1)}, bf16[1024,512]{1,0:T(8,128)(2,1)}) custom-call(s32[4]{0:T(128)} %pad_add_fusion.pos, bf16[8,1024,512]{2,1,0:T(8,128)(2,1)} %q0.7, bf16[4,1024,512]{2,1,0:T(8,128)(2,1)} %copy-done.1, bf16[4,3,128,256]{3,2,1,0:T(8,128)(2,1)} %copy-done.4, ...), custom_call_target="tpu_custom_call", output_to_operand_aliasing={{0}: (5, {})} | custom-call | flops 3221225472 | bytes 7340032 | tf_op jit(solution)/shard_map/apply_renewed/pallas_call | solution.py:117
  436.3 7.2 %apply_renewed.6 = (bf16[8,1024,512]{2,1,0:T(8,128)(2,1)}, bf16[1024,512]{1,0:T(8,128)(2,1)}) custom-call(s32[4]{0:T(128)} %pad_add_fusion.pos, bf16[8,1024,512]{2,1,0:T(8,128)(2,1)} %q0.7, bf16[4,1024,512]{2,1,0:T(8,128)(2,1)} %copy-done.1, bf16[4,3,128,256]{3,2,1,0:T(8,128)(2,1)} %copy-done.6, ...), custom_call_target="tpu_custom_call", output_to_operand_aliasing={{0}: (5, {})} | custom-call | flops 3221225472 | bytes 7340032 | tf_op jit(solution)/shard_map/apply_renewed/pallas_call | solution.py:117
  444.0 7.0 %apply_renewed.7 = (bf16[8,1024,512]{2,1,0:T(8,128)(2,1)}, bf16[1024,512]{1,0:T(8,128)(2,1)}) custom-call(s32[4]{0:T(128)} %pad_add_fusion.pos, bf16[8,1024,512]{2,1,0:T(8,128)(2,1)} %q0.7, bf16[4,1024,512]{2,1,0:T(8,128)(2,1)} %copy-done.1, bf16[4,3,128,256]{3,2,1,0:T(8,128)(2,1)} %copy-done.5, ...), custom_call_target="tpu_custom_call", output_to_operand_aliasing={{0}: (5, {})} | custom-call | flops 3221225472 | bytes 7340032 | tf_op jit(solution)/shard_map/apply_renewed/pallas_call | solution.py:117
  (383 shorter events, 258.0 us)
Async XLA Ops:
  4.8 98.5 %collective-permute-start.1 = (bf16[4,1024,512]{2,1,0:T(8,128)(2,1)}, bf16[4,1024,512]{2,1,0:T(8,128)(2,1)}, u32[]{:S(2)}, u32[]{:S(2)}) collective-permute-start(bf16[4,1024,512]{2,1,0:T(8,128)(2,1)} %constant_dynamic-slice_fusion.1), channel_id=1, source_target_pairs={{0,1},{1,0},{2,3},{3,2},{4,5},{5,4},{6,7},{7,6},{8,9},{9,8},{10,11... | collective-permute-start | bytes 12582920 | tf_op jit(solution)/shard_map/ppermute | solution.py:368
  13.8 91.0 %collective-permute-start.2 = (bf16[4,1024,512]{2,1,0:T(8,128)(2,1)}, bf16[4,1024,512]{2,1,0:T(8,128)(2,1)}, u32[]{:S(2)}, u32[]{:S(2)}) collective-permute-start(bf16[4,1024,512]{2,1,0:T(8,128)(2,1)} %constant_dynamic-slice_fusion), channel_id=1, source_target_pairs={{0,1},{1,0},{2,3},{3,2},{4,5},{5,4},{6,7},{7,6},{8,9},{9,8},{10,11... | collective-permute-start | bytes 12582920 | tf_op jit(solution)/shard_map/ppermute | solution.py:368
  100.2 318.9 %collective-permute-start = (bf16[4,1024,512]{2,1,0:T(8,128)(2,1)}, bf16[4,1024,512]{2,1,0:T(8,128)(2,1)S(1)}, u32[]{:S(2)}, u32[]{:S(2)}) collective-permute-start(bf16[4,1024,512]{2,1,0:T(8,128)(2,1)} %constant_dynamic-slice_fusion.2), channel_id=1, source_target_pairs={{0,1},{1,0},{2,3},{3,2},{4,5},{5,4},{6,7},{7,6},{8,9},{9,8},{10,11... | collective-permute-start | bytes 12582920 | tf_op jit(solution)/shard_map/ppermute | solution.py:368
  119.5 51.5 %collective-permute-start.71 = (bf16[4,3,64,256]{3,2,1,0:T(8,128)(2,1)S(1)}, bf16[4,3,64,256]{3,2,1,0:T(8,128)(2,1)S(1)}, u32[]{:S(2)}, u32[]{:S(2)}) collective-permute-start(bf16[4,3,64,256]{3,2,1,0:T(8,128)(2,1)S(1)} %pad_maximum_fusion.7.p0), channel_id=1, source_target_pairs={{0,16},{16,0},{1,17},{17,1},{2,18},{18,2},{3,19},{19,3},{4,20},{20... | collective-permute-start | bytes 1179656 | tf_op jit(solution)/shard_map/ppermute | solution.py:371
  121.7 50.2 %collective-permute-start.72 = (bf16[4,3,64,256]{3,2,1,0:T(8,128)(2,1)S(1)}, bf16[4,3,64,256]{3,2,1,0:T(8,128)(2,1)}, u32[]{:S(2)}, u32[]{:S(2)}) collective-permute-start(bf16[4,3,64,256]{3,2,1,0:T(8,128)(2,1)S(1)} %collective-permute-done.70.p1), channel_id=1, source_target_pairs={{0,16},{16,0},{1,17},{17,1},{2,18},{18,2},{3,19},{19,3},{4,20},{20... | collective-permute-start | bytes 1179656 | tf_op jit(solution)/shard_map/ppermute | solution.py:371
  123.2 32.2 %collective-permute-start.54 = (bf16[4,3,64,256]{3,2,1,0:T(8,128)(2,1)S(1)}, bf16[4,3,64,256]{3,2,1,0:T(8,128)(2,1)S(1)}, u32[]{:S(2)}, u32[]{:S(2)}) collective-permute-start(bf16[4,3,64,256]{3,2,1,0:T(8,128)(2,1)S(1)} %collective-permute-done.52.p1), channel_id=1, source_target_pairs={{0,16},{16,0},{1,17},{17,1},{2,18},{18,2},{3,19},{19,3},{4,20},{20... | collective-permute-start | bytes 1179656 | tf_op jit(solution)/shard_map/ppermute | solution.py:371
  140.1 47.5 %collective-permute-start.19 = (bf16[3,512,256]{2,1,0:T(8,128)(2,1)}, bf16[3,512,256]{2,1,0:T(8,128)(2,1)S(1)}, u32[]{:S(2)}, u32[]{:S(2)}) collective-permute-start(bf16[3,512,256]{2,1,0:T(8,128)(2,1)} %get-tuple-element.58), channel_id=1, source_target_pairs={{0,2},{2,0},{4,6},{6,4},{8,10},{10,8},{12,14},{14,12},{1,3},{3,1},... | collective-permute-start | bytes 2359304 | tf_op jit(solution)/shard_map/ppermute | solution.py:374
  155.4 36.4 %collective-permute-start.37 = (bf16[3,512,256]{2,1,0:T(8,128)(2,1)}, bf16[3,512,256]{2,1,0:T(8,128)(2,1)S(1)}, u32[]{:S(2)}, u32[]{:S(2)}) collective-permute-start(bf16[3,512,256]{2,1,0:T(8,128)(2,1)} %get-tuple-element.68), channel_id=1, source_target_pairs={{0,2},{2,0},{4,6},{6,4},{8,10},{10,8},{12,14},{14,12},{1,3},{3,1},... | collective-permute-start | bytes 2359304 | tf_op jit(solution)/shard_map/ppermute | solution.py:374
  171.1 22.8 %collective-permute-start.55 = (bf16[3,512,256]{2,1,0:T(8,128)(2,1)}, bf16[3,512,256]{2,1,0:T(8,128)(2,1)S(1)}, u32[]{:S(2)}, u32[]{:S(2)}) collective-permute-start(bf16[3,512,256]{2,1,0:T(8,128)(2,1)} %get-tuple-element.78), channel_id=1, source_target_pairs={{0,2},{2,0},{4,6},{6,4},{8,10},{10,8},{12,14},{14,12},{1,3},{3,1},... | collective-permute-start | bytes 2359304 | tf_op jit(solution)/shard_map/ppermute | solution.py:374
  186.3 21.4 %collective-permute-start.73 = (bf16[3,512,256]{2,1,0:T(8,128)(2,1)}, bf16[3,512,256]{2,1,0:T(8,128)(2,1)S(1)}, u32[]{:S(2)}, u32[]{:S(2)}) collective-permute-start(bf16[3,512,256]{2,1,0:T(8,128)(2,1)} %get-tuple-element.88), channel_id=1, source_target_pairs={{0,2},{2,0},{4,6},{6,4},{8,10},{10,8},{12,14},{14,12},{1,3},{3,1},... | collective-permute-start | bytes 2359304 | tf_op jit(solution)/shard_map/ppermute | solution.py:374
  191.8 21.3 %collective-permute-start.21 = (bf16[3,128,256]{2,1,0:T(8,128)(2,1)}, bf16[3,128,256]{2,1,0:T(8,128)(2,1)S(1)}, u32[]{:S(2)}, u32[]{:S(2)}) collective-permute-start(bf16[3,128,256]{2,1,0:T(8,128)(2,1)} %get-tuple-element.61), channel_id=1, source_target_pairs={{0,8},{2,10},{4,12},{6,14},{8,0},{10,2},{12,4},{14,6},{1,9},{3,11}... | collective-permute-start | bytes 589832 | tf_op jit(solution)/shard_map/ppermute | solution.py:374
  211.9 22.2 %collective-permute-start.39 = (bf16[3,128,256]{2,1,0:T(8,128)(2,1)}, bf16[3,128,256]{2,1,0:T(8,128)(2,1)S(1)}, u32[]{:S(2)}, u32[]{:S(2)}) collective-permute-start(bf16[3,128,256]{2,1,0:T(8,128)(2,1)} %get-tuple-element.71), channel_id=1, source_target_pairs={{0,8},{2,10},{4,12},{6,14},{8,0},{10,2},{12,4},{14,6},{1,9},{3,11}... | collective-permute-start | bytes 589832 | tf_op jit(solution)/shard_map/ppermute | solution.py:374
  213.1 22.5 %collective-permute-start.74 = (bf16[3,128,256]{2,1,0:T(8,128)(2,1)}, bf16[3,128,256]{2,1,0:T(8,128)(2,1)S(1)}, u32[]{:S(2)}, u32[]{:S(2)}) collective-permute-start(bf16[3,128,256]{2,1,0:T(8,128)(2,1)} %get-tuple-element.90), channel_id=1, source_target_pairs={{0,4},{2,6},{4,0},{6,2},{8,12},{10,14},{12,8},{14,10},{1,5},{3,7},... | collective-permute-start | bytes 589832 | tf_op jit(solution)/shard_map/ppermute | solution.py:374
  214.0 24.3 %collective-permute-start.75 = (bf16[3,128,256]{2,1,0:T(8,128)(2,1)}, bf16[3,128,256]{2,1,0:T(8,128)(2,1)S(1)}, u32[]{:S(2)}, u32[]{:S(2)}) collective-permute-start(bf16[3,128,256]{2,1,0:T(8,128)(2,1)} %get-tuple-element.91), channel_id=1, source_target_pairs={{0,8},{2,10},{4,12},{6,14},{8,0},{10,2},{12,4},{14,6},{1,9},{3,11}... | collective-permute-start | bytes 589832 | tf_op jit(solution)/shard_map/ppermute | solution.py:374
  216.0 22.5 %collective-permute-start.76 = (bf16[3,128,256]{2,1,0:T(8,128)(2,1)}, bf16[3,128,256]{2,1,0:T(8,128)(2,1)S(1)}, u32[]{:S(2)}, u32[]{:S(2)}) collective-permute-start(bf16[3,128,256]{2,1,0:T(8,128)(2,1)} %get-tuple-element.92), channel_id=1, source_target_pairs={{0,12},{2,14},{4,8},{6,10},{8,4},{10,6},{12,0},{14,2},{1,13},{3,15... | collective-permute-start | bytes 589832 | tf_op jit(solution)/shard_map/ppermute | solution.py:374
  238.3 23.2 %collective-permute-start.57 = (bf16[3,128,256]{2,1,0:T(8,128)(2,1)}, bf16[3,128,256]{2,1,0:T(8,128)(2,1)S(1)}, u32[]{:S(2)}, u32[]{:S(2)}) collective-permute-start(bf16[3,128,256]{2,1,0:T(8,128)(2,1)} %get-tuple-element.81), channel_id=1, source_target_pairs={{0,8},{2,10},{4,12},{6,14},{8,0},{10,2},{12,4},{14,6},{1,9},{3,11}... | collective-permute-start | bytes 589832 | tf_op jit(solution)/shard_map/ppermute | solution.py:374
  238.5 23.6 %collective-permute-start.58 = (bf16[3,128,256]{2,1,0:T(8,128)(2,1)}, bf16[3,128,256]{2,1,0:T(8,128)(2,1)S(1)}, u32[]{:S(2)}, u32[]{:S(2)}) collective-permute-start(bf16[3,128,256]{2,1,0:T(8,128)(2,1)} %get-tuple-element.82), channel_id=1, source_target_pairs={{0,12},{2,14},{4,8},{6,10},{8,4},{10,6},{12,0},{14,2},{1,13},{3,15... | collective-permute-start | bytes 589832 | tf_op jit(solution)/shard_map/ppermute | solution.py:374
  245.8 20.4 %collective-permute-start.23 = (f32[8,256]{1,0:T(8,128)}, f32[8,256]{1,0:T(8,128)S(1)}, u32[]{:S(2)}, u32[]{:S(2)}) collective-permute-start(f32[8,256]{1,0:T(8,128)} %get-tuple-element.66.sums_ref), channel_id=1, source_target_pairs={{0,2},{2,0},{4,6},{6,4},{8,10},{10,8},{12,14},{14,12},{1,3},{3,1},... | collective-permute-start | bytes 24584 | tf_op jit(solution)/shard_map/ppermute | solution.py:374
  282.6 97.7 %collective-permute-start.86 = (bf16[3,128,256]{2,1,0:T(8,128)(2,1)}, bf16[3,128,256]{2,1,0:T(8,128)(2,1)S(1)}, u32[]{:S(2)}, u32[]{:S(2)}) collective-permute-start(bf16[3,128,256]{2,1,0:T(8,128)(2,1)} %renewed_block.7), channel_id=1, source_target_pairs={{0,12},{2,14},{4,8},{6,10},{8,4},{10,6},{12,0},{14,2},{1,13},{3,15... | collective-permute-start | bytes 589832 | tf_op jit(solution)/shard_map/ppermute | solution.py:374
  284.2 99.4 %collective-permute-start.85 = (bf16[3,128,256]{2,1,0:T(8,128)(2,1)}, bf16[3,128,256]{2,1,0:T(8,128)(2,1)S(1)}, u32[]{:S(2)}, u32[]{:S(2)}) collective-permute-start(bf16[3,128,256]{2,1,0:T(8,128)(2,1)} %renewed_block.7), channel_id=1, source_target_pairs={{0,8},{2,10},{4,12},{6,14},{8,0},{10,2},{12,4},{14,6},{1,9},{3,11}... | collective-permute-start | bytes 589832 | tf_op jit(solution)/shard_map/ppermute | solution.py:374
  285.4 98.2 %collective-permute-start.84 = (bf16[3,128,256]{2,1,0:T(8,128)(2,1)}, bf16[3,128,256]{2,1,0:T(8,128)(2,1)S(1)}, u32[]{:S(2)}, u32[]{:S(2)}) collective-permute-start(bf16[3,128,256]{2,1,0:T(8,128)(2,1)} %renewed_block.7), channel_id=1, source_target_pairs={{0,4},{2,6},{4,0},{6,2},{8,12},{10,14},{12,8},{14,10},{1,5},{3,7},... | collective-permute-start | bytes 589832 | tf_op jit(solution)/shard_map/ppermute | solution.py:374
  385.8 33.3 %collective-permute-start.87 = (bf16[4,3,128,256]{3,2,1,0:T(8,128)(2,1)S(1)}, bf16[4,3,128,256]{3,2,1,0:T(8,128)(2,1)}, u32[]{:S(2)}, u32[]{:S(2)}) collective-permute-start(bf16[4,3,128,256]{3,2,1,0:T(8,128)(2,1)S(1)} %pad_maximum_fusion.3.h_ref), channel_id=1, source_target_pairs={{0,2},{2,0},{4,6},{6,4},{8,10},{10,8},{12,14},{14,12},{1,3},{3,1},... | collective-permute-start | bytes 2359304 | tf_op jit(solution)/shard_map/ppermute | solution.py:374
  403.8 24.5 %collective-permute-start.69 = (bf16[4,3,128,256]{3,2,1,0:T(8,128)(2,1)S(1)}, bf16[4,3,128,256]{3,2,1,0:T(8,128)(2,1)S(1)}, u32[]{:S(2)}, u32[]{:S(2)}) collective-permute-start(bf16[4,3,128,256]{3,2,1,0:T(8,128)(2,1)S(1)} %pad_maximum_fusion.2.h_ref), channel_id=1, source_target_pairs={{0,2},{2,0},{4,6},{6,4},{8,10},{10,8},{12,14},{14,12},{1,3},{3,1},... | collective-permute-start | bytes 2359304 | tf_op jit(solution)/shard_map/ppermute | solution.py:374
  418.0 26.0 %collective-permute-start.33 = (bf16[4,3,128,256]{3,2,1,0:T(8,128)(2,1)S(1)}, bf16[4,3,128,256]{3,2,1,0:T(8,128)(2,1)}, u32[]{:S(2)}, u32[]{:S(2)}) collective-permute-start(bf16[4,3,128,256]{3,2,1,0:T(8,128)(2,1)S(1)} %pad_maximum_fusion.h_ref), channel_id=1, source_target_pairs={{0,2},{2,0},{4,6},{6,4},{8,10},{10,8},{12,14},{14,12},{1,3},{3,1},... | collective-permute-start | bytes 2359304 | tf_op jit(solution)/shard_map/ppermute | solution.py:374
  (158 other events, 3251.8 us)

commit v2 on v0

--- a/solution.py
+++ b/solution.py
@@ -1,10 +1,17 @@
+import functools
+
 import jax
 import jax.numpy as jnp
 from jax import lax
+from jax.experimental import pallas as pl
+from jax.experimental.pallas import tpu as pltpu
 from jax.sharding import PartitionSpec as P
 
 EPSILON = 1e-06
 STEP_SIZE = 0.5
+BF16 = jnp.bfloat16
+F32 = jnp.float32
+VMEM_LIMIT = 56 * 1024 * 1024
 
 
 def column_squares(matrix):
@@ -46,7 +53,7 @@
     return (grad_gate, grad_up, grad_down)
 
 
-def on_device(queries, keys, values, lr_codes, fast_gate, fast_up, fast_down):
+def on_device_generic(queries, keys, values, lr_codes, fast_gate, fast_up, fast_down):
     token_rates = (lr_codes.astype(jnp.float32) + 1.0) / 16.0
     target = (-token_rates[:, :, None] * values.astype(jnp.float32)).astype(jnp.bfloat16)
     gate_b, up_b, down_b = (
@@ -94,7 +101,345 @@
     return apply_fast(queries, new_gate, new_up, new_down)
 
 
+CHUNKS = ((3,), (2,), (1, 0))
+
+
+def block(shape, index_map):
+    return pl.BlockSpec(shape, index_map)
+
+
+def whole(array):
+    return pl.BlockSpec(array.shape, lambda *_: (0,) * array.ndim)
+
+
+def anywhere():
+    return pl.BlockSpec(memory_space=pl.ANY)
+
+
+def call(body, name, positions, grid, operands, in_specs, out_shapes, out_specs, scratch=(), aliases=None, cost=None):
+    return pl.pallas_call(
+        body,
+        name=name,
+        out_shape=out_shapes,
+        grid_spec=pltpu.PrefetchScalarGridSpec(
+            num_scalar_prefetch=1,
+            grid=grid,
+            in_specs=in_specs,
+            out_specs=out_specs,
+            scratch_shapes=list(scratch),
+        ),
+        input_output_aliases=aliases or {},
+        compiler_params=pltpu.CompilerParams(vmem_limit_bytes=VMEM_LIMIT),
+        cost_estimate=cost,
+    )(positions, *operands)
+
+
+def sds(shape, dtype):
+    return jax.ShapeDtypeStruct(shape, dtype)
+
+
+def first_pieces(positions, own, received, chunk, after):
+    heads, rows, columns = own[0].shape
+    half, width = heads // 2, columns // 2
+
+    def body(pos, *refs):
+        mine = pl.ds(pl.multiple_of(pos[0] * rows, rows), rows)
+        theirs = pl.ds(pl.multiple_of((1 - pos[0]) * rows, rows), rows)
+        for j, out_ref in enumerate(refs[-half:]):
+            for i, k in enumerate(chunk):
+                head = pos[1] ^ (j ^ k)
+                for m in range(3):
+                    out_ref[i, m, mine, :] = refs[m][head].astype(BF16)
+                    out_ref[i, m, theirs, :] = refs[3 + m][head].astype(BF16)
+
+    spec = block((half, rows, width), lambda i, pos: (pos[0], 0, pos[3]))
+    shape = sds((len(chunk), 3, 2 * rows, width), BF16)
+    return call(
+        body, "first_pieces", positions, (1,), (*own, *received, *after),
+        [spec] * 6 + [anywhere()] * len(after), [shape] * half, [whole(shape)] * half,
+    )
+
+
+def gradients(positions, keys, values, rates, pieces, place_in_chunk, k, half, tile, after):
+    z_size, _, _, piece_rows, width = pieces[0].shape
+    rows, columns = z_size * 2 * piece_rows, 2 * width
+    tokens = keys[0].shape[1]
+    lanes = rates[0].shape[2]
+    steps = tokens // tile
+    last = k == 0
+
+    def body(pos, k0, k1, v0, v1, r0, r1, p0, p1, p2, p3, *rest):
+        keep, send = rest[len(after) : len(after) + 2]
+        w, total = rest[-2:]
+        step = pl.program_id(0)
+        z, x, y = pos[1], pos[2], pos[3]
+        mine = pl.ds(pl.multiple_of(x * width, 128), width)
+        theirs = pl.ds(pl.multiple_of((1 - x) * width, 128), width)
+
+        @pl.when(step == 0)
+        def _():
+            for ref, xx, yy in ((p0, x, y), (p1, 1 - x, y), (p2, x, 1 - y), (p3, 1 - x, 1 - y)):
+                cols = pl.ds(pl.multiple_of(yy * width, 128), width)
+                for j in range(z_size):
+                    at = pl.ds(pl.multiple_of((z ^ j) * 2 * piece_rows + xx * piece_rows, piece_rows), piece_rows)
+                    w[:, at, cols] = ref[j, 0]
+            if last:
+                own_w, squares = rest[len(after) + 2 : len(after) + 4]
+                own_w[...] = w[:, :, mine]
+                for m in range(3):
+                    full = w[m].astype(F32)
+                    squares[m : m + 1, :] = jnp.sum(full * full, axis=0, keepdims=True)
+
+        for n, (k_ref, v_ref, r_ref) in enumerate(((k0, v0, r0), (k1, v1, r1))):
+            key = k_ref[0]
+            rate = jnp.concatenate([r_ref[0].astype(F32)] * (columns // lanes), axis=1)
+            t = (-rate * v_ref[0].astype(F32)).astype(BF16)
+            gate = jnp.dot(key, w[0], preferred_element_type=F32)
+            up = jnp.dot(key, w[1], preferred_element_type=F32)
+            back = lax.dot_general(t, w[2], (((1,), (1,)), ((), ())), preferred_element_type=F32)
+            sig = 0.5 * jnp.tanh(0.5 * gate) + 0.5
+            silu = gate * sig
+            hidden = (silu * up).astype(BF16)
+            grad_up = (back * silu).astype(BF16)
+            grad_gate = (back * up * (sig + silu * (1.0 - sig))).astype(BF16)
+            for m, (a, b) in enumerate(((key, grad_gate), (key, grad_up), (hidden, t))):
+                part = lax.dot_general(a, b, (((0,), (0,)), ((), ())), preferred_element_type=F32)
+                if n == 0:
+                    @pl.when(step == 0)
+                    def _(m=m, part=part):
+                        total[m] = part
+
+                    @pl.when(step > 0)
+                    def _(m=m, part=part):
+                        total[m] += part
+                else:
+                    total[m] += part
+
+        @pl.when(step == steps - 1)
+        def _():
+            keep[...] = total[:, :, mine]
+            send[...] = total[:, :, theirs].astype(BF16)
+
+    at = lambda i, pos: (pos[0] * half + (pos[1] ^ k), i, 0)
+    rows_of, rates_of = block((1, tile, columns), at), block((1, tile, lanes), at)
+    piece = block((z_size, 1, 3, piece_rows, width), lambda i, pos: (0, place_in_chunk, 0, 0, 0))
+    outs = [sds((3, rows, width), F32), sds((3, rows, width), BF16)]
+    if last:
+        outs += [sds((3, rows, width), BF16), sds((8, columns), F32)]
+    return call(
+        body, "gradients", positions, (steps,),
+        (*keys, *values, *rates, *pieces, *after),
+        [rows_of] * 4 + [rates_of] * 2 + [piece] * 4 + [anywhere()] * len(after),
+        outs, [whole(o) for o in outs],
+        [pltpu.VMEM((3, rows, columns), BF16), pltpu.VMEM((3, rows, columns), F32)],
+        cost=pl.CostEstimate(flops=6 * 2 * 2 * tokens * rows * columns, bytes_accessed=14 * 2**20, transcendentals=2 * tokens * columns),
+    )
+
+
+def added(positions, keep, received, after):
+    def body(pos, keep_ref, *refs):
+        for m in range(3):
+            total = keep_ref[m]
+            for ref in refs[: len(received)]:
+                total = total + ref[m].astype(F32)
+            refs[-1][m] = total.astype(BF16)
+
+    operands = (keep, *received)
+    shape = sds(keep.shape, BF16)
+    specs = [whole(a) for a in operands] + [anywhere()] * len(after)
+    return call(body, "added", positions, (1,), (*operands, *after), specs, shape, whole(shape))
+
+
+def total_gradient(positions, keep, received):
+    def body(pos, keep_ref, *refs):
+        grad, sums = refs[-2:]
+        sums[...] = jnp.zeros_like(sums)
+        for m in range(3):
+            total = keep_ref[m]
+            for ref in refs[:-2]:
+                total = total + ref[m].astype(F32)
+            grad[m] = total
+            columns = jnp.sum(total * total, axis=0, keepdims=True)
+            sums[m : m + 1, :] = jnp.broadcast_to(jnp.sum(columns, axis=1, keepdims=True), (1, sums.shape[1]))
+
+    outs = [sds(keep.shape, F32), sds((8, 128), F32)]
+    operands = (keep, *received)
+    return call(body, "total_gradient", positions, (1,), operands, [whole(a) for a in operands], outs, [whole(o) for o in outs])
+
+
+def renewed_block(positions, grad, own_w, squares, sums, sums_in):
+    width = grad.shape[2]
+
+    def body(pos, g_ref, w_ref, sq_ref, sums_ref, sums_in_ref, out):
+        mine = pl.ds(pl.multiple_of(pos[2] * width, 128), width)
+        for m in range(3):
+            total_g = sums_ref[m : m + 1, :1] + sums_in_ref[m : m + 1, :1]
+            total_w = jnp.sum(sq_ref[m : m + 1, :], axis=1, keepdims=True)
+            scale = STEP_SIZE * jnp.sqrt(total_w + EPSILON) / jnp.sqrt(total_g + EPSILON)
+            moved = w_ref[m].astype(F32) - scale * g_ref[m]
+            col_moved = jnp.sum(moved * moved, axis=0, keepdims=True)
+            out[m] = (moved * jnp.sqrt((sq_ref[m : m + 1, mine] + EPSILON) / (col_moved + EPSILON))).astype(BF16)
+
+    operands = (grad, own_w, squares, sums, sums_in)
+    shape = sds(grad.shape, BF16)
+    return call(body, "renewed_block", positions, (1,), operands, [whole(a) for a in operands], shape, whole(shape))
+
+
+def apply_renewed(positions, queries, queries_in, held, swapped, k, half, tile, out):
+    _, rows, width = held.shape
+    columns = 2 * width
+    heads, tokens, _ = queries.shape
+    steps = tokens // tile
+
+    def body(pos, q0, q1, h_ref, s_ref, *refs):
+        out_ref, send_ref, w = refs[-3:]
+        x = pos[2]
+
+        @pl.when(pl.program_id(0) == 0)
+        def _():
+            w[:, :, pl.ds(pl.multiple_of(x * width, 128), width)] = h_ref[...]
+            w[:, :, pl.ds(pl.multiple_of((1 - x) * width, 128), width)] = s_ref[...]
+
+        for q_ref, is_own in ((q0, True), (q1, False)):
+            q = q_ref[0]
+            gate = jnp.dot(q, w[0], preferred_element_type=F32)
+            up = jnp.dot(q, w[1], preferred_element_type=F32)
+            hidden = (gate * (0.5 * jnp.tanh(0.5 * gate) + 0.5) * up).astype(BF16)
+            result = jnp.dot(hidden, w[2], preferred_element_type=F32).astype(BF16)
+            if is_own:
+                out_ref[0] = result
+            else:
+                send_ref[...] = result
+
+    here = block((1, tile, columns), lambda i, pos: (pos[0] * half + (pos[1] ^ k), i, 0))
+    operands = [queries, queries_in, held, swapped]
+    in_specs = [here, here, whole(held), whole(swapped)]
+    aliases = {}
+    if out is not None:
+        aliases = {1 + len(operands): 0}
+        operands.append(out)
+        in_specs.append(anywhere())
+    return call(
+        body, "apply_renewed", positions, (steps,), operands, in_specs,
+        [sds(queries.shape, BF16), sds((tokens, columns), BF16)],
+        [here, block((tile, columns), lambda i, pos: (i, 0))],
+        [pltpu.VMEM((3, rows, columns), BF16)],
+        aliases,
+        pl.CostEstimate(flops=3 * 2 * 2 * tokens * rows * columns, bytes_accessed=7 * 2**20, transcendentals=2 * tokens * columns),
+    )
+
+
+def place(positions, out, received, ks, half):
+    tokens, columns = received[0].shape
+
+    def body(pos, *refs):
+        for i in range(len(ks)):
+            @pl.when(pl.program_id(0) == i)
+            def _(i=i):
+                refs[-1][0] = refs[i][...]
+
+    def at(i, pos):
+        k = ks[0]
+        for n, other in enumerate(ks[1:], 1):
+            k = jnp.where(i == n, other, k)
+        return ((1 - pos[0]) * half + (pos[1] ^ k), 0, 0)
+
+    n = len(ks)
+    return call(
+        body, "place", positions, (n,), (*received, out), [whole(r) for r in received] + [anywhere()],
+        sds(out.shape, BF16), block((1, tokens, columns), at), aliases={1 + n: 0},
+    )
+
+
+def on_device_fast(queries, keys, values, lr_codes, fast_gate, fast_up, fast_down):
+    heads, tokens, _ = queries.shape
+    half = heads // 2
+    core, seq = lax.axis_index("sub"), lax.axis_index("seq")
+    positions = jnp.stack([core, seq // 2, seq % 2, lax.axis_index("groups")]).astype(jnp.int32)
+    flip = [(0, 1), (1, 0)]
+    tile = 512 if tokens % 512 == 0 else tokens
+
+    def over_sub(a):
+        return lax.ppermute(a, "sub", flip)
+
+    def over_groups(a):
+        return lax.ppermute(a, "groups", flip)
+
+    def over_x(a):
+        return lax.ppermute(a, "seq", [(i, i ^ 1) for i in range(8)])
+
+    def over_z(a, j):
+        return lax.ppermute(a, "seq", [(i, i ^ (2 * j)) for i in range(8)])
+
+    weights = (fast_gate, fast_up, fast_down)
+    rows_in = tuple(over_sub(w) for w in weights)
+    all_keys, all_values = (keys, over_sub(keys)), (values, over_sub(values))
+    rates = tuple(
+        jnp.broadcast_to(((codes.astype(F32) + 1.0) / 16.0).astype(BF16)[:, :, None], (*codes.shape, 128))
+        for codes in (lr_codes, over_sub(lr_codes))
+    )
+    queries_in = over_sub(queries)
+
+    def chunk_pieces(chunk, after):
+        own, *sends = first_pieces(positions, weights, rows_in, chunk, after)
+        return own, [over_z(a, j) for j, a in enumerate(sends, 1)]
+
+    pieces = {}
+
+    def chunk_spread(chunk, own, received):
+        held = jnp.stack((own, *received))
+        swapped = over_x(held)
+        everything = (held, swapped, over_groups(held), over_groups(swapped))
+        for i, k in enumerate(chunk):
+            pieces[k] = (everything, i)
+        return held
+
+    def head_gradients(k, after):
+        keep, send, *rest = gradients(positions, all_keys, all_values, rates, *pieces[k], k, half, tile, after)
+        return keep, over_x(send), *rest
+
+    first = chunk_pieces(CHUNKS[0], ())
+    second = chunk_pieces(CHUNKS[1], (first[0],))
+    held = chunk_spread(CHUNKS[0], *first)
+    third = chunk_pieces(CHUNKS[2], (second[0], held))
+    held = chunk_spread(CHUNKS[1], *second)
+    keep3, in3 = head_gradients(3, (third[0], held))
+    held = chunk_spread(CHUNKS[2], *third)
+    keep2, in2 = head_gradients(2, (keep3, held))
+    sum3 = added(positions, keep3, (in3,), (keep2,))
+    from1 = over_z(sum3, 1)
+    keep1, in1 = head_gradients(1, (sum3,))
+    sum2 = added(positions, keep2, (in2, from1), (keep1,))
+    from2 = over_z(sum2, 2)
+    keep0, in0, own_w, squares = head_gradients(0, (sum2,))
+    from1 = over_z(added(positions, keep1, (in1,), (keep0,)), 1)
+    grad, sums = total_gradient(positions, keep0, (in0, from1, from2))
+    renewed = renewed_block(positions, grad, own_w, squares, sums, over_x(sums))
+
+    matrices = {0: (renewed, over_x(renewed))}
+    from2 = over_z(renewed, 2)
+    from3 = over_z(from2, 1)
+    matrices[2] = (from2, over_x(from2))
+    matrices[1] = (over_z(renewed, 1), over_z(matrices[0][1], 1))
+    matrices[3] = (from3, over_x(from3))
+
+    out, returned = None, {}
+    for order in ((0, 2), (1, 3)):
+        for k in order:
+            out, sent = apply_renewed(positions, queries, queries_in, *matrices[k], k, half, tile, out)
+            returned[k] = over_sub(sent)
+        out = place(positions, out, [returned[k] for k in order], order, half)
+    return out
+
+
 def solution(mesh):
+    seq, sub, groups = mesh.shape["seq"], mesh.shape["sub"], mesh.shape["groups"]
+
+    def on_device(queries, *rest):
+        rows, columns = rest[3].shape[1:]
+        fits = (groups, seq, sub, queries.shape[0]) == (2, 8, 2, 8) and rows % 32 == 0 and columns == seq * sub * rows and columns % 256 == 0
+        return (on_device_fast if fits else on_device_generic)(queries, *rest)
+
     return jax.shard_map(
         on_device,
         mesh=mesh,

time: 795 us -> 356 us (0.45)
  waiting for transfers between devices: 472 us -> 159 us
  matrix products: 147 us -> 0 us
  Pallas kernels: 0 us -> 119 us
  blocking collectives: 118 us -> 0 us
  starting transfers between devices: 0.74 us -> 55 us
  other arithmetic: 20.9 us -> 4.29 us
  between operations: 13.3 us -> 0.19 us
    reduce_scatter x3 -> x0, waiting for transfers between devices: 247 us -> none  [the longest x1 107 us: on_device(): lax.psum_scatter(grad_gate, ('seq', 'sub'), scatter_dimension=1, tiled=True)]
    all_gather x6 -> x0, waiting for transfers between devices: 226 us -> none  [the longest x1 51.2 us: on_device(): lax.all_gather(renewed[1], ('seq', 'sub'), axis=1, tiled=True)]
    ppermute x0 -> x44, waiting for transfers between devices: none -> 159 us  [the longest x16 111 us: over_z(): return lax.ppermute(a, 'seq', [(i, i ^ 2 * j) for i in range(8)])]
    dot_general x8 -> x0, matrix products: 147 us -> none  [the longest x1 25.5 us: local_grads(): jnp.einsum('htd,htf->hdf', keys, grad_gate_pre, preferred_element_type=jn...]
    pallas_call x0 -> x18, Pallas kernels: none -> 119 us  [call(): pl.pallas_call(body, name=name, out_shape=out_shapes, grid_spec=pltpu.Pre...]
    psum x2 -> x0, blocking collectives: 118 us -> none  [the longest x1 60.4 us: on_device(): lax.psum((column_squares(fast_gate), column_squares(fast_up), column_squa...]
    ppermute x0 -> x44, starting transfers between devices: none -> 55 us  [the longest x16 33.4 us: over_z(): return lax.ppermute(a, 'seq', [(i, i ^ 2 * j) for i in range(8)])]
    dot_general x2 -> x0, local copies, waits for them, and re-layouts: 21.1 us -> none  [the longest x1 10.6 us: local_grads(): jnp.einsum('htd,htf->hdf', keys, grad_gate_pre, preferred_element_type=jn...]
  transfers between devices with their start and end apart: 9 -> 44, of which waited for: 9 -> 24; matrix products, arithmetic and copies ran while one was open for 20% -> 2% of each run, Pallas kernels for 0% -> 30%
where the time goes in v2:
time: 356 us; the launch traced here: 355 us
  waiting for transfers between devices  159 us (45%)
  Pallas kernels  119 us (33%)
  starting transfers between devices  55 us (15%)
  local copies, waits for them, and re-layouts  17.4 us (5%)
  other arithmetic  4.29 us (1%)
    pallas_call x18, Pallas kernels, call(): pl.pallas_call(body, name=name, out_shape=out_shapes, grid_spec=pltpu.Pre...  119 us
    ppermute x16, waiting for transfers between devices, over_z(): return lax.ppermute(a, 'seq', [(i, i ^ 2 * j) for i in range(8)])  111 us
    ppermute x16, starting transfers between devices, over_z(): return lax.ppermute(a, 'seq', [(i, i ^ 2 * j) for i in range(8)])  33.4 us
    ppermute x11, waiting for transfers between devices, over_sub(): return lax.ppermute(a, 'sub', flip)  22.7 us
    ppermute x11, waiting for transfers between devices, over_x(): return lax.ppermute(a, 'seq', [(i, i ^ 1) for i in range(8)])  14.9 us
    unnamed x76, local copies, waits for them, and re-layouts  13 us
    ppermute x11, starting transfers between devices, over_x(): return lax.ppermute(a, 'seq', [(i, i ^ 1) for i in range(8)])  12.3 us
    ppermute x6, waiting for transfers between devices, over_groups(): return lax.ppermute(a, 'groups', flip)  11.2 us
  transfers between devices with their start and end apart: 44, of which 24 were waited for; matrix products, arithmetic and copies ran while one was open for 2% of the time, Pallas kernels for 30%

profile of v2, /device:TPU:0, one launch (start us, length us, event | category | flops | bytes accessed | tf_op | source)
XLA Modules:
  0.0 355.0 jit_solution(7216996256058516339)
XLA Ops:
  1.5 11.0 %collective-permute-done.4.refs_3_ = f32[8,32,512]{2,1,0:T(8,128)S(1)} collective-permute-done((f32[8,32,512]{2,1,0:T(8,128)}, f32[8,32,512]{2,1,0:T(8,128)S(1)}, u32[]{:S(2)}, u32[]{:S(2)}) %collective-permute-start.4) | collective-permute-done | bytes 524320 | tf_op jit(solution)/shard_map/ppermute | solution.py:363
  22.9 4.9 %collective-permute-done.3 = s32[8,1024]{1,0:T(8,128)S(1)} collective-permute-done((s32[8,1024]{1,0:T(8,128)}, s32[8,1024]{1,0:T(8,128)S(1)}, u32[]{:S(2)}, u32[]{:S(2)}) %collective-permute-start.3) | collective-permute-done | bytes 32800 | tf_op jit(solution)/shard_map/ppermute | solution.py:363
  27.8 4.0 %collective-permute-start.8 = (bf16[1,3,64,256]{3,2,1,0:T(8,128)(2,1)}, bf16[1,3,64,256]{3,2,1,0:T(8,128)(2,1)S(1)}, u32[]{:S(2)}, u32[]{:S(2)}) collective-permute-start(bf16[1,3,64,256]{3,2,1,0:T(8,128)(2,1)} %get-tuple-element.40), channel_id=1, source_target_pairs={{0,8},{2,10},{4,12},{6,14},{8,0},{10,2},{12,4},{14,6},{1,9},{3,11}... | collective-permute-start | bytes 294920 | tf_op jit(solution)/shard_map/ppermute | solution.py:372
  35.8 4.0 %collective-permute-done.8 = bf16[1,3,64,256]{3,2,1,0:T(8,128)(2,1)S(1)} collective-permute-done((bf16[1,3,64,256]{3,2,1,0:T(8,128)(2,1)}, bf16[1,3,64,256]{3,2,1,0:T(8,128)(2,1)S(1)}, u32[]{:S(2)}, u32[]{:S(2)}) %collective-permute-start.8) | collective-permute-done | bytes 98336 | tf_op jit(solution)/shard_map/ppermute | solution.py:372
  50.4 6.9 %collective-permute-done.18 = bf16[1,3,64,256]{3,2,1,0:T(8,128)(2,1)S(1)} collective-permute-done((bf16[1,3,64,256]{3,2,1,0:T(8,128)(2,1)}, bf16[1,3,64,256]{3,2,1,0:T(8,128)(2,1)S(1)}, u32[]{:S(2)}, u32[]{:S(2)}) %collective-permute-start.18) | collective-permute-done | bytes 98336 | tf_op jit(solution)/shard_map/ppermute | solution.py:372
  59.6 6.0 %collective-permute-done.11 = bf16[2,3,64,256]{3,2,1,0:T(8,128)(2,1)S(1)} collective-permute-done((bf16[2,3,64,256]{3,2,1,0:T(8,128)(2,1)}, bf16[2,3,64,256]{3,2,1,0:T(8,128)(2,1)S(1)}, u32[]{:S(2)}, u32[]{:S(2)}) %collective-permute-start.11) | collective-permute-done | bytes 196640 | tf_op jit(solution)/shard_map/ppermute | solution.py:372
  99.1 14.1 %gradients.4 = (f32[3,512,256]{2,1,0:T(8,128)}, bf16[3,512,256]{2,1,0:T(8,128)(2,1)}) custom-call(s32[4]{0:T(128)} %pad_add_fusion.pos, bf16[8,1024,512]{2,1,0:T(8,128)(2,1)} %k0.7, bf16[8,1024,512]{2,1,0:T(8,128)(2,1)} %collective-permute-done.1.k1, bf16[8,1024,512]{2,1,0:T(8,128)(2,1)} %v0.7, bf16[8,1024,512]{2,1,0:T(8,128)(2,1)} %collective-permute-done.2.v1, ...), custom_call_target="tpu_custom_call" | custom-call | flops 6442450944 | bytes 14680064 | tf_op jit(solution)/shard_map/gradients/pallas_call | solution.py:120
  117.6 14.0 %gradients.5 = (f32[3,512,256]{2,1,0:T(8,128)}, bf16[3,512,256]{2,1,0:T(8,128)(2,1)}) custom-call(s32[4]{0:T(128)} %pad_add_fusion.pos, bf16[8,1024,512]{2,1,0:T(8,128)(2,1)} %k0.7, bf16[8,1024,512]{2,1,0:T(8,128)(2,1)} %collective-permute-done.1.k1, bf16[8,1024,512]{2,1,0:T(8,128)(2,1)} %v0.7, bf16[8,1024,512]{2,1,0:T(8,128)(2,1)} %collective-permute-done.2.v1, ...), custom_call_target="tpu_custom_call" | custom-call | flops 6442450944 | bytes 14680064 | tf_op jit(solution)/shard_map/gradients/pallas_call | solution.py:120
  136.4 3.9 %collective-permute-start.27 = (bf16[3,512,256]{2,1,0:T(8,128)(2,1)}, bf16[3,512,256]{2,1,0:T(8,128)(2,1)S(1)}, u32[]{:S(2)}, u32[]{:S(2)}) collective-permute-start(bf16[3,512,256]{2,1,0:T(8,128)(2,1)} %added.3.rest_0_), channel_id=1, source_target_pairs={{0,4},{2,6},{4,0},{6,2},{8,12},{10,14},{12,8},{14,10},{1,5},{3,7},... | collective-permute-start | bytes 2359304 | tf_op jit(solution)/shard_map/ppermute | solution.py:372
  140.3 6.0 %collective-permute-done.15.p3 = bf16[4,2,3,64,256]{4,3,2,1,0:T(8,128)(2,1)S(1)} collective-permute-done((bf16[4,2,3,64,256]{4,3,2,1,0:T(8,128)(2,1)S(1)}, bf16[4,2,3,64,256]{4,3,2,1,0:T(8,128)(2,1)S(1)}, u32[]{:S(2)}, u32[]{:S(2)}) %collective-permute-start.15) | collective-permute-done | bytes 786464 | tf_op jit(solution)/shard_map/ppermute | solution.py:366
  147.2 14.0 %gradients.6 = (f32[3,512,256]{2,1,0:T(8,128)}, bf16[3,512,256]{2,1,0:T(8,128)(2,1)}) custom-call(s32[4]{0:T(128)} %pad_add_fusion.pos, bf16[8,1024,512]{2,1,0:T(8,128)(2,1)} %k0.7, bf16[8,1024,512]{2,1,0:T(8,128)(2,1)} %collective-permute-done.1.k1, bf16[8,1024,512]{2,1,0:T(8,128)(2,1)} %v0.7, bf16[8,1024,512]{2,1,0:T(8,128)(2,1)} %collective-permute-done.2.v1, ...), custom_call_target="tpu_custom_call" | custom-call | flops 6442450944 | bytes 14680064 | tf_op jit(solution)/shard_map/gradients/pallas_call | solution.py:120
  166.6 14.3 %gradients.7 = (f32[3,512,256]{2,1,0:T(8,128)}, bf16[3,512,256]{2,1,0:T(8,128)(2,1)}, bf16[3,512,256]{2,1,0:T(8,128)(2,1)}, f32[8,512]{1,0:T(8,128)}) custom-call(s32[4]{0:T(128)} %pad_add_fusion.pos, bf16[8,1024,512]{2,1,0:T(8,128)(2,1)} %k0.7, bf16[8,1024,512]{2,1,0:T(8,128)(2,1)} %collective-permute-done.1.k1, bf16[8,1024,512]{2,1,0:T(8,128)(2,1)} %v0.7, ...), custom_call_target="tpu_custom_call" | custom-call | flops 6442450944 | bytes 14680064 | tf_op jit(solution)/shard_map/gradients/pallas_call | solution.py:120
  185.1 4.9 %collective-permute-start.30 = (bf16[3,512,256]{2,1,0:T(8,128)(2,1)}, bf16[3,512,256]{2,1,0:T(8,128)(2,1)S(1)}, u32[]{:S(2)}, u32[]{:S(2)}) collective-permute-start(bf16[3,512,256]{2,1,0:T(8,128)(2,1)} %added.5), channel_id=1, source_target_pairs={{0,4},{2,6},{4,0},{6,2},{8,12},{10,14},{12,8},{14,10},{1,5},{3,7},... | collective-permute-start | bytes 2359304 | tf_op jit(solution)/shard_map/ppermute | solution.py:372
  191.6 25.7 %collective-permute-done.30.refs_1_ = bf16[3,512,256]{2,1,0:T(8,128)(2,1)S(1)} collective-permute-done((bf16[3,512,256]{2,1,0:T(8,128)(2,1)}, bf16[3,512,256]{2,1,0:T(8,128)(2,1)S(1)}, u32[]{:S(2)}, u32[]{:S(2)}) %collective-permute-start.30) | collective-permute-done | bytes 786464 | tf_op jit(solution)/shard_map/ppermute | solution.py:372
  217.3 4.8 %collective-permute-done.31.refs_2_ = bf16[3,512,256]{2,1,0:T(8,128)(2,1)S(1)} collective-permute-done((bf16[3,512,256]{2,1,0:T(8,128)(2,1)S(1)}, bf16[3,512,256]{2,1,0:T(8,128)(2,1)S(1)}, u32[]{:S(2)}, u32[]{:S(2)}) %collective-permute-start.31) | collective-permute-done | bytes 786464 | tf_op jit(solution)/shard_map/ppermute | solution.py:372
  223.1 4.5 %total_gradient.1 = (f32[3,512,256]{2,1,0:T(8,128)}, f32[8,128]{1,0:T(8,128)}) custom-call(s32[4]{0:T(128)} %pad_add_fusion.pos, f32[3,512,256]{2,1,0:T(8,128)} %get-tuple-element.54.refs_1_.keep_ref, bf16[3,512,256]{2,1,0:T(8,128)(2,1)} %copy-done.23, bf16[3,512,256]{2,1,0:T(8,128)(2,1)} %copy-done.22, bf16[3,512,256]{2,1,0:T(8,128)(2,1)} %copy-done.24), custom_call_target="tpu_custom_call" | custom-call | tf_op jit(solution)/shard_map/total_gradient/pallas_call | solution.py:120
  237.3 29.3 %collective-permute-done.37.h_ref = bf16[3,512,256]{2,1,0:T(8,128)(2,1)S(1)} collective-permute-done((bf16[3,512,256]{2,1,0:T(8,128)(2,1)}, bf16[3,512,256]{2,1,0:T(8,128)(2,1)S(1)}, u32[]{:S(2)}, u32[]{:S(2)}) %collective-permute-start.37) | collective-permute-done | bytes 786464 | tf_op jit(solution)/shard_map/ppermute | solution.py:372
  269.3 7.3 %apply_renewed.4 = (bf16[8,1024,512]{2,1,0:T(8,128)(2,1)}, bf16[1024,512]{1,0:T(8,128)(2,1)}) custom-call(s32[4]{0:T(128)} %pad_add_fusion.pos, bf16[8,1024,512]{2,1,0:T(8,128)(2,1)} %q0.7, bf16[8,1024,512]{2,1,0:T(8,128)(2,1)} %collective-permute-done.q1, bf16[3,512,256]{2,1,0:T(8,128)(2,1)} %renewed_block.1.h_ref, bf16[3,512,256]{2,1,0:T(8,128)(2,1)} %copy-done.27), custom_call_target="tpu_custom_call" | custom-call | flops 3221225472 | bytes 7340032 | tf_op jit(solution)/shard_map/apply_renewed/pallas_call | solution.py:120
  277.5 6.7 %collective-permute-done.38.s_ref = bf16[3,512,256]{2,1,0:T(8,128)(2,1)S(1)} collective-permute-done((bf16[3,512,256]{2,1,0:T(8,128)(2,1)S(1)}, bf16[3,512,256]{2,1,0:T(8,128)(2,1)S(1)}, u32[]{:S(2)}, u32[]{:S(2)}) %collective-permute-start.38) | collective-permute-done | bytes 786464 | tf_op jit(solution)/shard_map/ppermute | solution.py:369
  285.1 7.1 %apply_renewed.5 = (bf16[8,1024,512]{2,1,0:T(8,128)(2,1)}, bf16[1024,512]{1,0:T(8,128)(2,1)}) custom-call(s32[4]{0:T(128)} %pad_add_fusion.pos, bf16[8,1024,512]{2,1,0:T(8,128)(2,1)} %q0.7, bf16[8,1024,512]{2,1,0:T(8,128)(2,1)} %collective-permute-done.q1, bf16[3,512,256]{2,1,0:T(8,128)(2,1)} %copy-done.15, ...), custom_call_target="tpu_custom_call", output_to_operand_aliasing={{0}: (5, {})} | custom-call | flops 3221225472 | bytes 7340032 | tf_op jit(solution)/shard_map/apply_renewed/pallas_call | solution.py:120
  301.8 11.8 %collective-permute-done.33.h_ref = bf16[3,512,256]{2,1,0:T(8,128)(2,1)S(1)} collective-permute-done((bf16[3,512,256]{2,1,0:T(8,128)(2,1)S(1)}, bf16[3,512,256]{2,1,0:T(8,128)(2,1)S(1)}, u32[]{:S(2)}, u32[]{:S(2)}) %collective-permute-start.33) | collective-permute-done | bytes 786464 | tf_op jit(solution)/shard_map/ppermute | solution.py:372
  313.6 16.6 %collective-permute-done.35.s_ref = bf16[3,512,256]{2,1,0:T(8,128)(2,1)S(1)} collective-permute-done((bf16[3,512,256]{2,1,0:T(8,128)(2,1)S(1)}, bf16[3,512,256]{2,1,0:T(8,128)(2,1)S(1)}, u32[]{:S(2)}, u32[]{:S(2)}) %collective-permute-start.35) | collective-permute-done | bytes 786464 | tf_op jit(solution)/shard_map/ppermute | solution.py:372
  331.2 7.0 %apply_renewed.6 = (bf16[8,1024,512]{2,1,0:T(8,128)(2,1)}, bf16[1024,512]{1,0:T(8,128)(2,1)}) custom-call(s32[4]{0:T(128)} %pad_add_fusion.pos, bf16[8,1024,512]{2,1,0:T(8,128)(2,1)} %q0.7, bf16[8,1024,512]{2,1,0:T(8,128)(2,1)} %collective-permute-done.q1, bf16[3,512,256]{2,1,0:T(8,128)(2,1)} %copy-done.16, ...), custom_call_target="tpu_custom_call", output_to_operand_aliasing={{0}: (5, {})} | custom-call | flops 3221225472 | bytes 7340032 | tf_op jit(solution)/shard_map/apply_renewed/pallas_call | solution.py:120
  339.2 7.1 %apply_renewed.7 = (bf16[8,1024,512]{2,1,0:T(8,128)(2,1)}, bf16[1024,512]{1,0:T(8,128)(2,1)}) custom-call(s32[4]{0:T(128)} %pad_add_fusion.pos, bf16[8,1024,512]{2,1,0:T(8,128)(2,1)} %q0.7, bf16[8,1024,512]{2,1,0:T(8,128)(2,1)} %collective-permute-done.q1, bf16[3,512,256]{2,1,0:T(8,128)(2,1)} %copy-done.14, ...), custom_call_target="tpu_custom_call", output_to_operand_aliasing={{0}: (5, {})} | custom-call | flops 3221225472 | bytes 7340032 | tf_op jit(solution)/shard_map/apply_renewed/pallas_call | solution.py:120
  (166 shorter events, 118.8 us)
Async XLA Ops:
  0.0 94.2 %collective-permute-start.1 = (bf16[8,1024,512]{2,1,0:T(8,128)(2,1)}, bf16[8,1024,512]{2,1,0:T(8,128)(2,1)}, u32[]{:S(2)}, u32[]{:S(2)}) collective-permute-start(bf16[8,1024,512]{2,1,0:T(8,128)(2,1)} %k0.7), channel_id=1, source_target_pairs={{0,1},{1,0},{2,3},{3,2},{4,5},{5,4},{6,7},{7,6},{8,9},{9,8},{10,11... | collective-permute-start | bytes 25165832 | tf_op jit(solution)/shard_map/ppermute | solution.py:363
  0.5 94.2 %collective-permute-start.2 = (bf16[8,1024,512]{2,1,0:T(8,128)(2,1)}, bf16[8,1024,512]{2,1,0:T(8,128)(2,1)}, u32[]{:S(2)}, u32[]{:S(2)}) collective-permute-start(bf16[8,1024,512]{2,1,0:T(8,128)(2,1)} %v0.7), channel_id=1, source_target_pairs={{0,1},{1,0},{2,3},{3,2},{4,5},{5,4},{6,7},{7,6},{8,9},{9,8},{10,11... | collective-permute-start | bytes 25165832 | tf_op jit(solution)/shard_map/ppermute | solution.py:363
  0.5 267.8 %collective-permute-start = (bf16[8,1024,512]{2,1,0:T(8,128)(2,1)}, bf16[8,1024,512]{2,1,0:T(8,128)(2,1)}, u32[]{:S(2)}, u32[]{:S(2)}) collective-permute-start(bf16[8,1024,512]{2,1,0:T(8,128)(2,1)} %q0.7), channel_id=1, source_target_pairs={{0,1},{1,0},{2,3},{3,2},{4,5},{5,4},{6,7},{7,6},{8,9},{9,8},{10,11... | collective-permute-start | bytes 25165832 | tf_op jit(solution)/shard_map/ppermute | solution.py:363
  48.5 17.1 %collective-permute-start.11 = (bf16[2,3,64,256]{3,2,1,0:T(8,128)(2,1)}, bf16[2,3,64,256]{3,2,1,0:T(8,128)(2,1)S(1)}, u32[]{:S(2)}, u32[]{:S(2)}) collective-permute-start(bf16[2,3,64,256]{3,2,1,0:T(8,128)(2,1)} %get-tuple-element.44), channel_id=1, source_target_pairs={{0,8},{2,10},{4,12},{6,14},{8,0},{10,2},{12,4},{14,6},{1,9},{3,11}... | collective-permute-start | bytes 589832 | tf_op jit(solution)/shard_map/ppermute | solution.py:372
  88.6 27.8 %collective-permute-start.13 = (bf16[4,2,3,64,256]{4,3,2,1,0:T(8,128)(2,1)S(1)}, bf16[4,2,3,64,256]{4,3,2,1,0:T(8,128)(2,1)S(1)}, u32[]{:S(2)}, u32[]{:S(2)}) collective-permute-start(bf16[4,2,3,64,256]{4,3,2,1,0:T(8,128)(2,1)S(1)} %pad_maximum_fusion.rest_1_.p0), channel_id=1, source_target_pairs={{0,2},{2,0},{4,6},{6,4},{8,10},{10,8},{12,14},{14,12},{1,3},{3,1},... | collective-permute-start | bytes 2359304 | tf_op jit(solution)/shard_map/ppermute | solution.py:369
  92.6 22.1 %collective-permute-start.20 = (bf16[4,1,3,64,256]{4,3,2,1,0:T(8,128)(2,1)S(1)}, bf16[4,1,3,64,256]{4,3,2,1,0:T(8,128)(2,1)S(1)}, u32[]{:S(2)}, u32[]{:S(2)}) collective-permute-start(bf16[4,1,3,64,256]{4,3,2,1,0:T(8,128)(2,1)S(1)} %pad_maximum_fusion.2.rest_1_.p0), channel_id=1, source_target_pairs={{0,16},{16,0},{1,17},{17,1},{2,18},{18,2},{3,19},{19,3},{4,20},{20... | collective-permute-start | bytes 1179656 | tf_op jit(solution)/shard_map/ppermute | solution.py:366
  94.2 22.7 %collective-permute-start.21 = (bf16[4,1,3,64,256]{4,3,2,1,0:T(8,128)(2,1)S(1)}, bf16[4,1,3,64,256]{4,3,2,1,0:T(8,128)(2,1)S(1)}, u32[]{:S(2)}, u32[]{:S(2)}) collective-permute-start(bf16[4,1,3,64,256]{4,3,2,1,0:T(8,128)(2,1)S(1)} %collective-permute-done.19.p1), channel_id=1, source_target_pairs={{0,16},{16,0},{1,17},{17,1},{2,18},{18,2},{3,19},{19,3},{4,20},{20... | collective-permute-start | bytes 1179656 | tf_op jit(solution)/shard_map/ppermute | solution.py:366
  113.2 19.0 %collective-permute-start.26 = (bf16[3,512,256]{2,1,0:T(8,128)(2,1)}, bf16[3,512,256]{2,1,0:T(8,128)(2,1)S(1)}, u32[]{:S(2)}, u32[]{:S(2)}) collective-permute-start(bf16[3,512,256]{2,1,0:T(8,128)(2,1)} %get-tuple-element.52), channel_id=1, source_target_pairs={{0,2},{2,0},{4,6},{6,4},{8,10},{10,8},{12,14},{14,12},{1,3},{3,1},... | collective-permute-start | bytes 2359304 | tf_op jit(solution)/shard_map/ppermute | solution.py:369
  114.8 25.5 %collective-permute-start.14 = (bf16[4,2,3,64,256]{4,3,2,1,0:T(8,128)(2,1)S(1)}, bf16[4,2,3,64,256]{4,3,2,1,0:T(8,128)(2,1)S(1)}, u32[]{:S(2)}, u32[]{:S(2)}) collective-permute-start(bf16[4,2,3,64,256]{4,3,2,1,0:T(8,128)(2,1)S(1)} %pad_maximum_fusion.rest_1_.p0), channel_id=1, source_target_pairs={{0,16},{16,0},{1,17},{17,1},{2,18},{18,2},{3,19},{19,3},{4,20},{20... | collective-permute-start | bytes 2359304 | tf_op jit(solution)/shard_map/ppermute | solution.py:366
  116.3 30.0 %collective-permute-start.15 = (bf16[4,2,3,64,256]{4,3,2,1,0:T(8,128)(2,1)S(1)}, bf16[4,2,3,64,256]{4,3,2,1,0:T(8,128)(2,1)S(1)}, u32[]{:S(2)}, u32[]{:S(2)}) collective-permute-start(bf16[4,2,3,64,256]{4,3,2,1,0:T(8,128)(2,1)S(1)} %collective-permute-done.13.p1), channel_id=1, source_target_pairs={{0,16},{16,0},{1,17},{17,1},{2,18},{18,2},{3,19},{19,3},{4,20},{20... | collective-permute-start | bytes 2359304 | tf_op jit(solution)/shard_map/ppermute | solution.py:366
  131.6 30.2 %collective-permute-start.25 = (bf16[3,512,256]{2,1,0:T(8,128)(2,1)}, bf16[3,512,256]{2,1,0:T(8,128)(2,1)S(1)}, u32[]{:S(2)}, u32[]{:S(2)}) collective-permute-start(bf16[3,512,256]{2,1,0:T(8,128)(2,1)} %get-tuple-element.51), channel_id=1, source_target_pairs={{0,2},{2,0},{4,6},{6,4},{8,10},{10,8},{12,14},{14,12},{1,3},{3,1},... | collective-permute-start | bytes 2359304 | tf_op jit(solution)/shard_map/ppermute | solution.py:369
  136.4 25.4 %collective-permute-start.27 = (bf16[3,512,256]{2,1,0:T(8,128)(2,1)}, bf16[3,512,256]{2,1,0:T(8,128)(2,1)S(1)}, u32[]{:S(2)}, u32[]{:S(2)}) collective-permute-start(bf16[3,512,256]{2,1,0:T(8,128)(2,1)} %added.3.rest_0_), channel_id=1, source_target_pairs={{0,4},{2,6},{4,0},{6,2},{8,12},{10,14},{12,8},{14,10},{1,5},{3,7},... | collective-permute-start | bytes 2359304 | tf_op jit(solution)/shard_map/ppermute | solution.py:372
  161.2 19.6 %collective-permute-start.29 = (bf16[3,512,256]{2,1,0:T(8,128)(2,1)}, bf16[3,512,256]{2,1,0:T(8,128)(2,1)S(1)}, u32[]{:S(2)}, u32[]{:S(2)}) collective-permute-start(bf16[3,512,256]{2,1,0:T(8,128)(2,1)} %get-tuple-element.56), channel_id=1, source_target_pairs={{0,2},{2,0},{4,6},{6,4},{8,10},{10,8},{12,14},{14,12},{1,3},{3,1},... | collective-permute-start | bytes 2359304 | tf_op jit(solution)/shard_map/ppermute | solution.py:369
  185.1 32.3 %collective-permute-start.30 = (bf16[3,512,256]{2,1,0:T(8,128)(2,1)}, bf16[3,512,256]{2,1,0:T(8,128)(2,1)S(1)}, u32[]{:S(2)}, u32[]{:S(2)}) collective-permute-start(bf16[3,512,256]{2,1,0:T(8,128)(2,1)} %added.5), channel_id=1, source_target_pairs={{0,4},{2,6},{4,0},{6,2},{8,12},{10,14},{12,8},{14,10},{1,5},{3,7},... | collective-permute-start | bytes 2359304 | tf_op jit(solution)/shard_map/ppermute | solution.py:372
  190.0 27.4 %collective-permute-start.28 = (bf16[3,512,256]{2,1,0:T(8,128)(2,1)}, bf16[3,512,256]{2,1,0:T(8,128)(2,1)S(1)}, u32[]{:S(2)}, u32[]{:S(2)}) collective-permute-start(bf16[3,512,256]{2,1,0:T(8,128)(2,1)} %get-tuple-element.55), channel_id=1, source_target_pairs={{0,2},{2,0},{4,6},{6,4},{8,10},{10,8},{12,14},{14,12},{1,3},{3,1},... | collective-permute-start | bytes 2359304 | tf_op jit(solution)/shard_map/ppermute | solution.py:369
  190.5 31.7 %collective-permute-start.31 = (bf16[3,512,256]{2,1,0:T(8,128)(2,1)S(1)}, bf16[3,512,256]{2,1,0:T(8,128)(2,1)S(1)}, u32[]{:S(2)}, u32[]{:S(2)}) collective-permute-start(bf16[3,512,256]{2,1,0:T(8,128)(2,1)S(1)} %copy-done.6), channel_id=1, source_target_pairs={{0,8},{2,10},{4,12},{6,14},{8,0},{10,2},{12,4},{14,6},{1,9},{3,11}... | collective-permute-start | bytes 2359304 | tf_op jit(solution)/shard_map/ppermute | solution.py:372
  235.8 30.8 %collective-permute-start.37 = (bf16[3,512,256]{2,1,0:T(8,128)(2,1)}, bf16[3,512,256]{2,1,0:T(8,128)(2,1)S(1)}, u32[]{:S(2)}, u32[]{:S(2)}) collective-permute-start(bf16[3,512,256]{2,1,0:T(8,128)(2,1)} %renewed_block.1.h_ref), channel_id=1, source_target_pairs={{0,8},{2,10},{4,12},{6,14},{8,0},{10,2},{12,4},{14,6},{1,9},{3,11}... | collective-permute-start | bytes 2359304 | tf_op jit(solution)/shard_map/ppermute | solution.py:372
  236.0 32.4 %collective-permute-start.34 = (bf16[3,512,256]{2,1,0:T(8,128)(2,1)}, bf16[3,512,256]{2,1,0:T(8,128)(2,1)S(1)}, u32[]{:S(2)}, u32[]{:S(2)}) collective-permute-start(bf16[3,512,256]{2,1,0:T(8,128)(2,1)} %renewed_block.1.h_ref), channel_id=1, source_target_pairs={{0,2},{2,0},{4,6},{6,4},{8,10},{10,8},{12,14},{14,12},{1,3},{3,1},... | collective-permute-start | bytes 2359304 | tf_op jit(solution)/shard_map/ppermute | solution.py:369
  266.6 17.6 %collective-permute-start.38 = (bf16[3,512,256]{2,1,0:T(8,128)(2,1)S(1)}, bf16[3,512,256]{2,1,0:T(8,128)(2,1)S(1)}, u32[]{:S(2)}, u32[]{:S(2)}) collective-permute-start(bf16[3,512,256]{2,1,0:T(8,128)(2,1)S(1)} %collective-permute-done.37.h_ref), channel_id=1, source_target_pairs={{0,2},{2,0},{4,6},{6,4},{8,10},{10,8},{12,14},{14,12},{1,3},{3,1},... | collective-permute-start | bytes 2359304 | tf_op jit(solution)/shard_map/ppermute | solution.py:369
  276.6 20.2 %collective-permute-start.36 = (bf16[1024,512]{1,0:T(8,128)(2,1)}, bf16[1024,512]{1,0:T(8,128)(2,1)S(1)}, u32[]{:S(2)}, u32[]{:S(2)}) collective-permute-start(bf16[1024,512]{1,0:T(8,128)(2,1)} %get-tuple-element.61), channel_id=1, source_target_pairs={{0,1},{1,0},{2,3},{3,2},{4,5},{5,4},{6,7},{7,6},{8,9},{9,8},{10,11... | collective-permute-start | bytes 3145736 | tf_op jit(solution)/shard_map/ppermute | solution.py:363
  276.6 20.2 %collective-permute-start.41 = (bf16[3,512,256]{2,1,0:T(8,128)(2,1)S(1)}, bf16[3,512,256]{2,1,0:T(8,128)(2,1)S(1)}, u32[]{:S(2)}, u32[]{:S(2)}) collective-permute-start(bf16[3,512,256]{2,1,0:T(8,128)(2,1)S(1)} %collective-permute-done.37.h_ref), channel_id=1, source_target_pairs={{0,4},{2,6},{4,0},{6,2},{8,12},{10,14},{12,8},{14,10},{1,5},{3,7},... | collective-permute-start | bytes 2359304 | tf_op jit(solution)/shard_map/ppermute | solution.py:372
  292.2 21.4 %collective-permute-start.33 = (bf16[3,512,256]{2,1,0:T(8,128)(2,1)S(1)}, bf16[3,512,256]{2,1,0:T(8,128)(2,1)S(1)}, u32[]{:S(2)}, u32[]{:S(2)}) collective-permute-start(bf16[3,512,256]{2,1,0:T(8,128)(2,1)S(1)} %copy-done.5), channel_id=1, source_target_pairs={{0,4},{2,6},{4,0},{6,2},{8,12},{10,14},{12,8},{14,10},{1,5},{3,7},... | collective-permute-start | bytes 2359304 | tf_op jit(solution)/shard_map/ppermute | solution.py:372
  295.0 35.3 %collective-permute-start.35 = (bf16[3,512,256]{2,1,0:T(8,128)(2,1)S(1)}, bf16[3,512,256]{2,1,0:T(8,128)(2,1)S(1)}, u32[]{:S(2)}, u32[]{:S(2)}) collective-permute-start(bf16[3,512,256]{2,1,0:T(8,128)(2,1)S(1)} %copy-done.28), channel_id=1, source_target_pairs={{0,4},{2,6},{4,0},{6,2},{8,12},{10,14},{12,8},{14,10},{1,5},{3,7},... | collective-permute-start | bytes 2359304 | tf_op jit(solution)/shard_map/ppermute | solution.py:372
  296.7 41.5 %collective-permute-start.42 = (bf16[3,512,256]{2,1,0:T(8,128)(2,1)S(1)}, bf16[3,512,256]{2,1,0:T(8,128)(2,1)S(1)}, u32[]{:S(2)}, u32[]{:S(2)}) collective-permute-start(bf16[3,512,256]{2,1,0:T(8,128)(2,1)S(1)} %collective-permute-done.41.h_ref), channel_id=1, source_target_pairs={{0,2},{2,0},{4,6},{6,4},{8,10},{10,8},{12,14},{14,12},{1,3},{3,1},... | collective-permute-start | bytes 2359304 | tf_op jit(solution)/shard_map/ppermute | solution.py:369
  (58 other events, 540.7 us)

commit v3 on v2

--- a/solution.py
+++ b/solution.py
@@ -11,7 +11,7 @@
 STEP_SIZE = 0.5
 BF16 = jnp.bfloat16
 F32 = jnp.float32
-VMEM_LIMIT = 56 * 1024 * 1024
+VMEM_LIMIT = 64 * 1024 * 1024
 
 
 def column_squares(matrix):
@@ -101,9 +101,6 @@
     return apply_fast(queries, new_gate, new_up, new_down)
 
 
-CHUNKS = ((3,), (2,), (1, 0))
-
-
 def block(shape, index_map):
     return pl.BlockSpec(shape, index_map)
 
@@ -116,7 +113,7 @@
     return pl.BlockSpec(memory_space=pl.ANY)
 
 
-def call(body, name, positions, grid, operands, in_specs, out_shapes, out_specs, scratch=(), aliases=None, cost=None):
+def call(body, name, positions, grid, operands, in_specs, out_shapes, out_specs, scratch=(), aliases=None, estimate=None, vmem=VMEM_LIMIT):
     return pl.pallas_call(
         body,
         name=name,
@@ -129,8 +126,8 @@
             scratch_shapes=list(scratch),
         ),
         input_output_aliases=aliases or {},
-        compiler_params=pltpu.CompilerParams(vmem_limit_bytes=VMEM_LIMIT),
-        cost_estimate=cost,
+        compiler_params=pltpu.CompilerParams(vmem_limit_bytes=vmem),
+        cost_estimate=estimate,
     )(positions, *operands)
 
 
@@ -138,38 +135,98 @@
     return jax.ShapeDtypeStruct(shape, dtype)
 
 
-def first_pieces(positions, own, received, chunk, after):
+def cost(microseconds):
+    return pl.CostEstimate(flops=0, bytes_accessed=int(microseconds * 3e6), transcendentals=0)
+
+
+def first_pieces(positions, own, received, k, after):
     heads, rows, columns = own[0].shape
     half, width = heads // 2, columns // 2
 
     def body(pos, *refs):
         mine = pl.ds(pl.multiple_of(pos[0] * rows, rows), rows)
         theirs = pl.ds(pl.multiple_of((1 - pos[0]) * rows, rows), rows)
-        for j, out_ref in enumerate(refs[-half:]):
-            for i, k in enumerate(chunk):
-                head = pos[1] ^ (j ^ k)
-                for m in range(3):
-                    out_ref[i, m, mine, :] = refs[m][head].astype(BF16)
-                    out_ref[i, m, theirs, :] = refs[3 + m][head].astype(BF16)
+        everything, sends = refs[-half - 1], refs[-half:]
+        for head in range(half):
+            for m in range(3):
+                everything[head, m, mine, :] = refs[m][head].astype(BF16)
+                everything[head, m, theirs, :] = refs[3 + m][head].astype(BF16)
+        for j, out_ref in enumerate(sends):
+            out_ref[...] = everything[pos[1] ^ (j ^ k)]
 
     spec = block((half, rows, width), lambda i, pos: (pos[0], 0, pos[3]))
-    shape = sds((len(chunk), 3, 2 * rows, width), BF16)
+    outs = [sds((half, 3, 2 * rows, width), BF16)] + [sds((3, 2 * rows, width), BF16)] * half
     return call(
         body, "first_pieces", positions, (1,), (*own, *received, *after),
-        [spec] * 6 + [anywhere()] * len(after), [shape] * half, [whole(shape)] * half,
-    )
-
-
-def gradients(positions, keys, values, rates, pieces, place_in_chunk, k, half, tile, after):
-    z_size, _, _, piece_rows, width = pieces[0].shape
-    rows, columns = z_size * 2 * piece_rows, 2 * width
+        [spec] * 6 + [anywhere()] * len(after), outs, [whole(o) for o in outs], vmem=60 * 1024 * 1024,
+    )
+
+
+def next_pieces(positions, arrived, rows, k, after, handed=None):
+    half = len(arrived)
+    more = [] if k is None else list(rows)
+
+    passed = [] if handed is None else [handed]
+
+    def body(pos, *refs):
+        held, *sends = refs[half + len(more) + len(after) + len(passed) :]
+        for j in range(half):
+            held[j] = refs[j][...]
+        if more:
+            height = rows[0].shape[2]
+            for ref, x in ((refs[half], pos[2]), (refs[half + 1], 1 - pos[2])):
+                at = pl.ds(pl.multiple_of(x * height, height), height)
+                for j in range(half):
+                    sends[j][:, at, :] = ref[pos[1] ^ (j ^ k)]
+
+    outs = [sds((half, *arrived[0].shape), BF16)]
+    if more:
+        outs += [sds((3, 2 * rows[0].shape[2], rows[0].shape[3]), BF16)] * half
+    operands = (*arrived, *more)
+    others = (*after, *passed)
+    aliases = {len(operands) + len(others): len(outs)} if passed else {}
+    return call(
+        body, "next_pieces", positions, (1,), (*operands, *others),
+        [whole(a) for a in operands] + [anywhere()] * len(others),
+        outs + [sds(p.shape, p.dtype) for p in passed], [whole(o) for o in outs] + [anywhere() for _ in passed],
+        aliases=aliases, estimate=cost(3),
+    )
+
+
+def copied(positions, array, after):
+    def body(pos, in_ref, *rest):
+        rest[-1][...] = in_ref[...]
+
+    shape = sds(array.shape, BF16)
+    return call(body, "copied", positions, (1,), (array, *after), [whole(array)] + [anywhere()] * len(after), shape, whole(shape))
+
+
+def other_half(positions, array, half, after):
+    def body(pos, in_ref, *rest):
+        rest[-1][...] = in_ref[...]
+
+    _, tokens, columns = array.shape
+    spec = block((1, tokens // 2, columns), lambda i, j, pos: ((1 - pos[0]) * half + i, j, 0))
+    out = block((1, tokens // 2, columns), lambda i, j, pos: (i, j, 0))
+    return call(
+        body, "other_half", positions, (half, 2), (array, *after), [spec] + [anywhere()] * len(after),
+        sds((half, tokens, columns), BF16), out, estimate=cost(3),
+    )
+
+
+def gradients(positions, keys, values, rates, pieces, k, half, tile, after, cuts):
+    z_size, _, piece_rows, width = pieces[0].shape
+    columns = keys[0].shape[2]
+    rows = columns
+    quarter = rows // z_size
     tokens = keys[0].shape[1]
     lanes = rates[0].shape[2]
     steps = tokens // tile
     last = k == 0
 
-    def body(pos, k0, k1, v0, v1, r0, r1, p0, p1, p2, p3, *rest):
-        keep, send = rest[len(after) : len(after) + 2]
+    def body(pos, k0, k1, v0, v1, r0, r1, *rest):
+        parts, rest = rest[: len(pieces)], rest[len(pieces) + len(after) :]
+        keep, sends = rest[0], rest[1 : 1 + cuts]
         w, total = rest[-2:]
         step = pl.program_id(0)
         z, x, y = pos[1], pos[2], pos[3]
@@ -178,13 +235,14 @@
 
         @pl.when(step == 0)
         def _():
-            for ref, xx, yy in ((p0, x, y), (p1, 1 - x, y), (p2, x, 1 - y), (p3, 1 - x, 1 - y)):
+            places = ((0, y), (0, 1 - y)) if len(parts) == 2 else ((x, y), (1 - x, y), (x, 1 - y), (1 - x, 1 - y))
+            for ref, (xx, yy) in zip(parts, places):
                 cols = pl.ds(pl.multiple_of(yy * width, 128), width)
                 for j in range(z_size):
-                    at = pl.ds(pl.multiple_of((z ^ j) * 2 * piece_rows + xx * piece_rows, piece_rows), piece_rows)
-                    w[:, at, cols] = ref[j, 0]
+                    at = pl.ds(pl.multiple_of((z ^ j) * quarter + xx * piece_rows, piece_rows), piece_rows)
+                    w[:, at, cols] = ref[j]
             if last:
-                own_w, squares = rest[len(after) + 2 : len(after) + 4]
+                own_w, squares = rest[1 + cuts : 3 + cuts]
                 own_w[...] = w[:, :, mine]
                 for m in range(3):
                     full = w[m].astype(F32)
@@ -218,36 +276,40 @@
         @pl.when(step == steps - 1)
         def _():
             keep[...] = total[:, :, mine]
-            send[...] = total[:, :, theirs].astype(BF16)
+            for c in range(cuts):
+                sends[c][...] = total[:, c * (rows // cuts) : (c + 1) * (rows // cuts), theirs].astype(BF16)
 
     at = lambda i, pos: (pos[0] * half + (pos[1] ^ k), i, 0)
     rows_of, rates_of = block((1, tile, columns), at), block((1, tile, lanes), at)
-    piece = block((z_size, 1, 3, piece_rows, width), lambda i, pos: (0, place_in_chunk, 0, 0, 0))
-    outs = [sds((3, rows, width), F32), sds((3, rows, width), BF16)]
+    outs = [sds((3, rows, width), F32)] + [sds((3, rows // cuts, width), BF16)] * cuts
     if last:
         outs += [sds((3, rows, width), BF16), sds((8, columns), F32)]
     return call(
         body, "gradients", positions, (steps,),
         (*keys, *values, *rates, *pieces, *after),
-        [rows_of] * 4 + [rates_of] * 2 + [piece] * 4 + [anywhere()] * len(after),
+        [rows_of] * 4 + [rates_of] * 2 + [whole(p) for p in pieces] + [anywhere()] * len(after),
         outs, [whole(o) for o in outs],
         [pltpu.VMEM((3, rows, columns), BF16), pltpu.VMEM((3, rows, columns), F32)],
-        cost=pl.CostEstimate(flops=6 * 2 * 2 * tokens * rows * columns, bytes_accessed=14 * 2**20, transcendentals=2 * tokens * columns),
-    )
-
-
-def added(positions, keep, received, after):
+        estimate=pl.CostEstimate(flops=6 * 2 * 2 * tokens * rows * columns, bytes_accessed=14 * 2**20, transcendentals=2 * tokens * columns),
+    )
+
+
+def added(positions, keep, received, after, dtype=BF16, microseconds=1, cuts=1):
+    rows = keep.shape[1]
+
     def body(pos, keep_ref, *refs):
         for m in range(3):
-            total = keep_ref[m]
-            for ref in refs[: len(received)]:
-                total = total + ref[m].astype(F32)
-            refs[-1][m] = total.astype(BF16)
+            for c in range(cuts):
+                at = pl.ds(c * (rows // cuts), rows // cuts)
+                total = keep_ref[m, at, :] + refs[c][m].astype(F32)
+                for ref in refs[cuts : len(received)]:
+                    total = total + ref[m, at, :].astype(F32)
+                refs[-1][m, at, :] = total.astype(dtype)
 
     operands = (keep, *received)
-    shape = sds(keep.shape, BF16)
+    shape = sds(keep.shape, dtype)
     specs = [whole(a) for a in operands] + [anywhere()] * len(after)
-    return call(body, "added", positions, (1,), (*operands, *after), specs, shape, whole(shape))
+    return call(body, "added", positions, (1,), (*operands, *after), specs, shape, whole(shape), estimate=cost(microseconds))
 
 
 def total_gradient(positions, keep, received):
@@ -285,18 +347,31 @@
     return call(body, "renewed_block", positions, (1,), operands, [whole(a) for a in operands], shape, whole(shape))
 
 
-def apply_renewed(positions, queries, queries_in, held, swapped, k, half, tile, out):
+def apply_renewed(positions, queries, queries_in, held, swapped, k, half, tile, out, late, after):
     _, rows, width = held.shape
     columns = 2 * width
     heads, tokens, _ = queries.shape
     steps = tokens // tile
+    blocks = [b for _, b in late]
+    first = len(after) + len(blocks) + (0 if out is None else 1)
 
     def body(pos, q0, q1, h_ref, s_ref, *refs):
-        out_ref, send_ref, w = refs[-3:]
-        x = pos[2]
-
-        @pl.when(pl.program_id(0) == 0)
+        late_refs = refs[: len(blocks)]
+        out_ref, send_ref, w, result, sems, late_sems = refs[first:]
+        x, step = pos[2], pl.program_id(0)
+
+        def placed(i):
+            head = pos[0] * half + (pos[1] ^ k)
+            return pltpu.make_async_copy(result.at[i], out_ref.at[head, pl.ds(i * tile, tile)], sems.at[i])
+
+        def brought(i):
+            head = (1 - pos[0]) * half + (pos[1] ^ late[i][0])
+            return pltpu.make_async_copy(late_refs[i], out_ref.at[head], late_sems.at[i])
+
+        @pl.when(step == 0)
         def _():
+            for i in range(len(blocks)):
+                brought(i).start()
             w[:, :, pl.ds(pl.multiple_of(x * width, 128), width)] = h_ref[...]
             w[:, :, pl.ds(pl.multiple_of((1 - x) * width, 128), width)] = s_ref[...]
 
@@ -305,15 +380,27 @@
             gate = jnp.dot(q, w[0], preferred_element_type=F32)
             up = jnp.dot(q, w[1], preferred_element_type=F32)
             hidden = (gate * (0.5 * jnp.tanh(0.5 * gate) + 0.5) * up).astype(BF16)
-            result = jnp.dot(hidden, w[2], preferred_element_type=F32).astype(BF16)
+            values = jnp.dot(hidden, w[2], preferred_element_type=F32).astype(BF16)
             if is_own:
-                out_ref[0] = result
+                for i in range(steps):
+                    @pl.when(step == i)
+                    def _(i=i, values=values):
+                        result[i] = values
+                        placed(i).start()
             else:
-                send_ref[...] = result
+                send_ref[...] = values
+
+        @pl.when(step == steps - 1)
+        def _():
+            for i in range(steps):
+                placed(i).wait()
+            for i in range(len(blocks)):
+                brought(i).wait()
 
     here = block((1, tile, columns), lambda i, pos: (pos[0] * half + (pos[1] ^ k), i, 0))
-    operands = [queries, queries_in, held, swapped]
-    in_specs = [here, here, whole(held), whole(swapped)]
+    there = block((1, tile, columns), lambda i, pos: (pos[1] ^ k, i, 0))
+    operands = [queries, queries_in, held, swapped, *blocks, *after]
+    in_specs = [here, there, whole(held), whole(swapped)] + [whole(b) for b in blocks] + [anywhere()] * len(after)
     aliases = {}
     if out is not None:
         aliases = {1 + len(operands): 0}
@@ -322,32 +409,33 @@
     return call(
         body, "apply_renewed", positions, (steps,), operands, in_specs,
         [sds(queries.shape, BF16), sds((tokens, columns), BF16)],
-        [here, block((tile, columns), lambda i, pos: (i, 0))],
-        [pltpu.VMEM((3, rows, columns), BF16)],
+        [anywhere(), block((tile, columns), lambda i, pos: (i, 0))],
+        [
+            pltpu.VMEM((3, rows, columns), BF16), pltpu.VMEM((steps, tile, columns), BF16),
+            pltpu.SemaphoreType.DMA((steps,)), pltpu.SemaphoreType.DMA((max(len(blocks), 1),)),
+        ],
         aliases,
         pl.CostEstimate(flops=3 * 2 * 2 * tokens * rows * columns, bytes_accessed=7 * 2**20, transcendentals=2 * tokens * columns),
     )
 
 
-def place(positions, out, received, ks, half):
-    tokens, columns = received[0].shape
+def place(positions, out, late, half):
+    n = len(late)
 
     def body(pos, *refs):
-        for i in range(len(ks)):
-            @pl.when(pl.program_id(0) == i)
-            def _(i=i):
-                refs[-1][0] = refs[i][...]
-
-    def at(i, pos):
-        k = ks[0]
-        for n, other in enumerate(ks[1:], 1):
-            k = jnp.where(i == n, other, k)
-        return ((1 - pos[0]) * half + (pos[1] ^ k), 0, 0)
-
-    n = len(ks)
+        out_ref, sems = refs[-2:]
+        copies = [
+            pltpu.make_async_copy(refs[i], out_ref.at[(1 - pos[0]) * half + (pos[1] ^ k)], sems.at[i])
+            for i, (k, _) in enumerate(late)
+        ]
+        for copy in copies:
+            copy.start()
+        for copy in copies:
+            copy.wait()
+
     return call(
-        body, "place", positions, (n,), (*received, out), [whole(r) for r in received] + [anywhere()],
-        sds(out.shape, BF16), block((1, tokens, columns), at), aliases={1 + n: 0},
+        body, "place", positions, (1,), (*(b for _, b in late), out), [whole(b) for _, b in late] + [anywhere()],
+        sds(out.shape, BF16), anywhere(), [pltpu.SemaphoreType.DMA((n,))], {1 + n: 0}, cost(1),
     )
 
 
@@ -378,58 +466,58 @@
         jnp.broadcast_to(((codes.astype(F32) + 1.0) / 16.0).astype(BF16)[:, :, None], (*codes.shape, 128))
         for codes in (lr_codes, over_sub(lr_codes))
     )
-    queries_in = over_sub(queries)
-
-    def chunk_pieces(chunk, after):
-        own, *sends = first_pieces(positions, weights, rows_in, chunk, after)
-        return own, [over_z(a, j) for j, a in enumerate(sends, 1)]
-
-    pieces = {}
-
-    def chunk_spread(chunk, own, received):
-        held = jnp.stack((own, *received))
-        swapped = over_x(held)
-        everything = (held, swapped, over_groups(held), over_groups(swapped))
-        for i, k in enumerate(chunk):
-            pieces[k] = (everything, i)
-        return held
-
-    def head_gradients(k, after):
-        keep, send, *rest = gradients(positions, all_keys, all_values, rates, *pieces[k], k, half, tile, after)
+    def head_gradients(k, pieces, after):
+        keep, send, *rest = gradients(positions, all_keys, all_values, rates, pieces, k, half, tile, after, 1)
         return keep, over_x(send), *rest
 
-    first = chunk_pieces(CHUNKS[0], ())
-    second = chunk_pieces(CHUNKS[1], (first[0],))
-    held = chunk_spread(CHUNKS[0], *first)
-    third = chunk_pieces(CHUNKS[2], (second[0], held))
-    held = chunk_spread(CHUNKS[1], *second)
-    keep3, in3 = head_gradients(3, (third[0], held))
-    held = chunk_spread(CHUNKS[2], *third)
-    keep2, in2 = head_gradients(2, (keep3, held))
-    sum3 = added(positions, keep3, (in3,), (keep2,))
+    def turn(pieces, k, after, handed=None):
+        arrived = (pieces[0], *(over_z(a, j) for j, a in enumerate(pieces[1:], 1)))
+        return next_pieces(positions, arrived, rows, k, after, handed)
+
+    everything, *pieces = first_pieces(positions, weights, rows_in, 3, ())
+    rows = (everything, over_x(everything))
+    held, *pieces = turn(pieces, 2, ())
+    swapped = over_x(held)
+    pieces3 = (held, swapped, over_groups(held), over_groups(swapped))
+    sent_queries = other_half(positions, queries, half, (held,))
+    queries_in = over_sub(sent_queries)
+    held, *pieces = turn(pieces, 1, (*pieces3, sent_queries, *rates))
+    pieces2 = (held, over_groups(held))
+    keep3, *sends = gradients(positions, all_keys, all_values, rates, pieces3, 3, half, tile, (held,), 4)
+    in3 = [over_x(a) for a in sends]
+    held, *pieces = turn(pieces, 0, (keep3, pieces2[1]))
+    pieces1 = (held, over_groups(held))
+    sum3 = added(positions, keep3, in3, (held,), cuts=4)
     from1 = over_z(sum3, 1)
-    keep1, in1 = head_gradients(1, (sum3,))
-    sum2 = added(positions, keep2, (in2, from1), (keep1,))
+    keep2, in2 = head_gradients(2, pieces2, (sum3,))
+    (held,) = turn(pieces, None, (keep2, pieces1[1]))
+    pieces0 = (held, over_groups(held))
+    keep1, in1 = head_gradients(1, pieces1, (held,))
+    sum2 = added(positions, keep2, (in2, from1), (keep1, pieces0[1]))
     from2 = over_z(sum2, 2)
-    keep0, in0, own_w, squares = head_gradients(0, (sum2,))
-    from1 = over_z(added(positions, keep1, (in1,), (keep0,)), 1)
-    grad, sums = total_gradient(positions, keep0, (in0, from1, from2))
+    keep0, in0, own_w, squares = head_gradients(0, pieces0, (sum2,))
+    sum1 = added(positions, keep1, (in1,), (keep0,))
+    from1 = over_z(sum1, 1)
+    partial = added(positions, keep0, (from2,), (sum1,), F32, 8)
+    grad, sums = total_gradient(positions, partial, (in0, from1))
     renewed = renewed_block(positions, grad, own_w, squares, sums, over_x(sums))
 
-    matrices = {0: (renewed, over_x(renewed))}
-    from2 = over_z(renewed, 2)
+    swapped = over_x(renewed)
+    from1, from2 = over_z(renewed, 1), over_z(renewed, 2)
     from3 = over_z(from2, 1)
-    matrices[2] = (from2, over_x(from2))
-    matrices[1] = (over_z(renewed, 1), over_z(matrices[0][1], 1))
-    matrices[3] = (from3, over_x(from3))
-
-    out, returned = None, {}
-    for order in ((0, 2), (1, 3)):
-        for k in order:
-            out, sent = apply_renewed(positions, queries, queries_in, *matrices[k], k, half, tile, out)
-            returned[k] = over_sub(sent)
-        out = place(positions, out, [returned[k] for k in order], order, half)
-    return out
+    matrices = {0: (renewed, swapped), 2: (from2, over_x(from2)), 3: (from3, over_x(from3))}
+
+    def head_output(k, out, late, after):
+        out, sent = apply_renewed(positions, queries, queries_in, *matrices[k], k, half, tile, out, late, after)
+        return out, (k, over_sub(sent))
+
+    out, late0 = head_output(0, None, (), (from1, from2))
+    swapped_late = copied(positions, swapped, (from3, out))
+    matrices[1] = (from1, over_z(swapped_late, 1))
+    out, late2 = head_output(2, out, (), (swapped_late,))
+    out, late1 = head_output(1, out, (late0,), matrices[3])
+    out, late3 = head_output(3, out, (late2,), ())
+    return place(positions, out, (late1, late3), half)
 
 
 def solution(mesh):

time: 356 us -> 311 us (0.87)
  waiting for transfers between devices: 159 us -> 111 us
  Pallas kernels: 119 us -> 138 us
  local copies, waits for them, and re-layouts: 17.4 us -> 6.71 us
  starting transfers between devices: 55 us -> 51 us
    ppermute x16 -> x19, waiting for transfers between devices: 111 us -> 77.8 us  [over_z(): return lax.ppermute(a, 'seq', [(i, i ^ 2 * j) for i in range(8)])]
    pallas_call x18 -> x22, Pallas kernels: 119 us -> 138 us  [call(): pl.pallas_call(body, name=name, out_shape=out_shapes, grid_spec=pltpu.Pre...]
    unnamed x76 -> x6, local copies, waits for them, and re-layouts: 13 us -> 0.83 us
    ppermute x6 -> x5, waiting for transfers between devices: 11.2 us -> 0.01 us  [over_groups(): return lax.ppermute(a, 'groups', flip)]
    ppermute x11, waiting for transfers between devices: 22.7 us -> 13 us  [over_sub(): return lax.ppermute(a, 'sub', flip)]
    ppermute x16 -> x19, starting transfers between devices: 33.4 us -> 26.1 us  [over_z(): return lax.ppermute(a, 'seq', [(i, i ^ 2 * j) for i in range(8)])]
    ppermute x11 -> x13, waiting for transfers between devices: 14.9 us -> 20.6 us  [over_x(): return lax.ppermute(a, 'seq', [(i, i ^ 1) for i in range(8)])]
    ppermute x11 -> x13, starting transfers between devices: 12.3 us -> 17.1 us  [over_x(): return lax.ppermute(a, 'seq', [(i, i ^ 1) for i in range(8)])]
  transfers between devices with their start and end apart: 44 -> 48, of which waited for: 24 -> 20; matrix products, arithmetic and copies ran while one was open for 2% -> 3% of each run, Pallas kernels for 30% -> 43%
where the time goes in v3:
time: 311 us; the launch traced here: 310 us
  Pallas kernels  138 us (44%)
  waiting for transfers between devices  111 us (36%)
  starting transfers between devices  51 us (16%)
  local copies, waits for them, and re-layouts  6.71 us (2%)
    pallas_call x22, Pallas kernels, call(): pl.pallas_call(body, name=name, out_shape=out_shapes, grid_spec=pltpu.Pre...  138 us
    ppermute x19, waiting for transfers between devices, over_z(): return lax.ppermute(a, 'seq', [(i, i ^ 2 * j) for i in range(8)])  77.8 us
    ppermute x19, starting transfers between devices, over_z(): return lax.ppermute(a, 'seq', [(i, i ^ 2 * j) for i in range(8)])  26.1 us
    ppermute x13, waiting for transfers between devices, over_x(): return lax.ppermute(a, 'seq', [(i, i ^ 1) for i in range(8)])  20.6 us
    ppermute x13, starting transfers between devices, over_x(): return lax.ppermute(a, 'seq', [(i, i ^ 1) for i in range(8)])  17.1 us
    ppermute x11, waiting for transfers between devices, over_sub(): return lax.ppermute(a, 'sub', flip)  13 us
  transfers between devices with their start and end apart: 48, of which 20 were waited for; matrix products, arithmetic and copies ran while one was open for 3% of the time, Pallas kernels for 43%

profile of v3, /device:TPU:0, one launch (start us, length us, event | category | flops | bytes accessed | tf_op | source)
XLA Modules:
  0.0 310.1 jit_solution(15288031213964384360)
XLA Ops:
  2.1 6.0 %collective-permute-done.refs_3_ = f32[8,32,512]{2,1,0:T(8,128)S(1)} collective-permute-done((f32[8,32,512]{2,1,0:T(8,128)}, f32[8,32,512]{2,1,0:T(8,128)S(1)}, u32[]{:S(2)}, u32[]{:S(2)}) %collective-permute-start) | collective-permute-done | bytes 524320 | tf_op jit(solution)/shard_map/ppermute | solution.py:451
  22.5 4.7 %collective-permute-start.5 = (bf16[3,64,256]{2,1,0:T(8,128)(2,1)}, bf16[3,64,256]{2,1,0:T(8,128)(2,1)}, u32[]{:S(2)}, u32[]{:S(2)}) collective-permute-start(bf16[3,64,256]{2,1,0:T(8,128)(2,1)} %get-tuple-element.51), channel_id=1, source_target_pairs={{0,12},{2,14},{4,8},{6,10},{8,4},{10,6},{12,0},{14,2},{1,13},{3,15... | collective-permute-start | bytes 294920 | tf_op jit(solution)/shard_map/ppermute | solution.py:460
  44.9 5.8 %collective-permute-done.12.refs_2_ = bf16[3,128,256]{2,1,0:T(8,128)(2,1)} collective-permute-done((bf16[3,128,256]{2,1,0:T(8,128)(2,1)}, bf16[3,128,256]{2,1,0:T(8,128)(2,1)}, u32[]{:S(2)}, u32[]{:S(2)}) %collective-permute-start.12) | collective-permute-done | bytes 196640 | tf_op jit(solution)/shard_map/ppermute | solution.py:460
  53.3 7.3 %other_half.1.refs_10_ = bf16[4,1024,512]{2,1,0:T(8,128)(2,1)} custom-call(s32[4]{0:T(128)} %pad_add_fusion.pos, bf16[8,1024,512]{2,1,0:T(8,128)(2,1)} %q0.7, bf16[4,3,64,256]{3,2,1,0:T(8,128)(2,1)} %get-tuple-element.53.rest_0_.refs_6_), custom_call_target="tpu_custom_call" | custom-call | bytes 9000000 | tf_op jit(solution)/shard_map/other_half/pallas_call | solution.py:117
  66.5 3.4 %next_pieces.5 = (bf16[4,3,128,256]{3,2,1,0:T(8,128)(2,1)}, bf16[3,128,256]{2,1,0:T(8,128)(2,1)}, bf16[3,128,256]{2,1,0:T(8,128)(2,1)}, bf16[3,128,256]{2,1,0:T(8,128)(2,1)}, bf16[3,128,256]{2,1,0:T(8,128)(2,1)}) custom-call(s32[4]{0:T(128)} %pad_add_fusion.pos, bf16[3,128,256]{2,1,0:T(8,128)(2,1)} %get-tuple-element.54.refs_0_, ...), custom_call_target="tpu_custom_call" | custom-call | bytes 9000000 | tf_op jit(solution)/shard_map/next_pieces/pallas_call | solution.py:117
  75.7 14.0 %gradients.4 = (f32[3,512,256]{2,1,0:T(8,128)}, bf16[3,128,256]{2,1,0:T(8,128)(2,1)}, bf16[3,128,256]{2,1,0:T(8,128)(2,1)}, bf16[3,128,256]{2,1,0:T(8,128)(2,1)}, bf16[3,128,256]{2,1,0:T(8,128)(2,1)}) custom-call(s32[4]{0:T(128)} %pad_add_fusion.pos, bf16[8,1024,512]{2,1,0:T(8,128)(2,1)} %k0.7, bf16[8,1024,512]{2,1,0:T(8,128)(2,1)} %collective-permute-done.8.k1, ...), custom_call_target="tpu_custom_call" | custom-call | flops 6442450944 | bytes 14680064 | tf_op jit(solution)/shard_map/gradients/pallas_call | solution.py:117
  98.0 4.2 %collective-permute-done.25.refs_1_ = bf16[3,128,256]{2,1,0:T(8,128)(2,1)} collective-permute-done((bf16[3,128,256]{2,1,0:T(8,128)(2,1)}, bf16[3,128,256]{2,1,0:T(8,128)(2,1)}, u32[]{:S(2)}, u32[]{:S(2)}) %collective-permute-start.25) | collective-permute-done | bytes 196640 | tf_op jit(solution)/shard_map/ppermute | solution.py:457
  111.7 14.0 %gradients.5 = (f32[3,512,256]{2,1,0:T(8,128)}, bf16[3,512,256]{2,1,0:T(8,128)(2,1)}) custom-call(s32[4]{0:T(128)} %pad_add_fusion.pos, bf16[8,1024,512]{2,1,0:T(8,128)(2,1)} %k0.7, bf16[8,1024,512]{2,1,0:T(8,128)(2,1)} %collective-permute-done.8.k1, bf16[8,1024,512]{2,1,0:T(8,128)(2,1)} %v0.7, bf16[8,1024,512]{2,1,0:T(8,128)(2,1)} %collective-permute-done.9.v1, ...), custom_call_target="tpu_custom_call" | custom-call | flops 6442450944 | bytes 14680064 | tf_op jit(solution)/shard_map/gradients/pallas_call | solution.py:117
  130.7 14.2 %gradients.6 = (f32[3,512,256]{2,1,0:T(8,128)}, bf16[3,512,256]{2,1,0:T(8,128)(2,1)}) custom-call(s32[4]{0:T(128)} %pad_add_fusion.pos, bf16[8,1024,512]{2,1,0:T(8,128)(2,1)} %k0.7, bf16[8,1024,512]{2,1,0:T(8,128)(2,1)} %collective-permute-done.8.k1, bf16[8,1024,512]{2,1,0:T(8,128)(2,1)} %v0.7, bf16[8,1024,512]{2,1,0:T(8,128)(2,1)} %collective-permute-done.9.v1, ...), custom_call_target="tpu_custom_call" | custom-call | flops 6442450944 | bytes 14680064 | tf_op jit(solution)/shard_map/gradients/pallas_call | solution.py:117
  145.4 3.6 %added.5.rest_2_ = bf16[3,512,256]{2,1,0:T(8,128)(2,1)} custom-call(s32[4]{0:T(128)} %pad_add_fusion.pos, f32[3,512,256]{2,1,0:T(8,128)} %get-tuple-element.73.refs_4_.keep_ref, bf16[3,512,256]{2,1,0:T(8,128)(2,1)} %collective-permute-done.30.refs_0_, bf16[3,512,256]{2,1,0:T(8,128)(2,1)} %collective-permute-done.31.refs_1_, ...), custom_call_target="tpu_custom_call" | custom-call | bytes 3000000 | tf_op jit(solution)/shard_map/added/pallas_call | solution.py:117
  151.5 14.5 %gradients.7 = (f32[3,512,256]{2,1,0:T(8,128)}, bf16[3,512,256]{2,1,0:T(8,128)(2,1)}, bf16[3,512,256]{2,1,0:T(8,128)(2,1)}, f32[8,512]{1,0:T(8,128)}) custom-call(s32[4]{0:T(128)} %pad_add_fusion.pos, bf16[8,1024,512]{2,1,0:T(8,128)(2,1)} %k0.7, bf16[8,1024,512]{2,1,0:T(8,128)(2,1)} %collective-permute-done.8.k1, bf16[8,1024,512]{2,1,0:T(8,128)(2,1)} %v0.7, ...), custom_call_target="tpu_custom_call" | custom-call | flops 6442450944 | bytes 14680064 | tf_op jit(solution)/shard_map/gradients/pallas_call | solution.py:117
  170.8 10.7 %collective-permute-done.32.refs_0_ = bf16[3,512,256]{2,1,0:T(8,128)(2,1)} collective-permute-done((bf16[3,512,256]{2,1,0:T(8,128)(2,1)}, bf16[3,512,256]{2,1,0:T(8,128)(2,1)}, u32[]{:S(2)}, u32[]{:S(2)}) %collective-permute-start.32) | collective-permute-done | bytes 786464 | tf_op jit(solution)/shard_map/ppermute | solution.py:460
  181.6 3.6 %added.7.keep_ref = f32[3,512,256]{2,1,0:T(8,128)} custom-call(s32[4]{0:T(128)} %pad_add_fusion.pos, f32[3,512,256]{2,1,0:T(8,128)} %get-tuple-element.76.refs_1_.keep_ref, bf16[3,512,256]{2,1,0:T(8,128)(2,1)} %collective-permute-done.32.refs_0_, bf16[3,512,256]{2,1,0:T(8,128)(2,1)} %added.6.refs_1_), custom_call_target="tpu_custom_call" | custom-call | bytes 24000000 | tf_op jit(solution)/shard_map/added/pallas_call | solution.py:117
  185.2 13.1 %collective-permute-done.35.refs_1_ = bf16[3,512,256]{2,1,0:T(8,128)(2,1)} collective-permute-done((bf16[3,512,256]{2,1,0:T(8,128)(2,1)}, bf16[3,512,256]{2,1,0:T(8,128)(2,1)}, u32[]{:S(2)}, u32[]{:S(2)}) %collective-permute-start.35) | collective-permute-done | bytes 786464 | tf_op jit(solution)/shard_map/ppermute | solution.py:460
  198.3 4.2 %total_gradient.1 = (f32[3,512,256]{2,1,0:T(8,128)}, f32[8,128]{1,0:T(8,128)}) custom-call(s32[4]{0:T(128)} %pad_add_fusion.pos, f32[3,512,256]{2,1,0:T(8,128)} %added.7.keep_ref, bf16[3,512,256]{2,1,0:T(8,128)(2,1)} %collective-permute-done.34.refs_0_, bf16[3,512,256]{2,1,0:T(8,128)(2,1)} %collective-permute-done.35.refs_1_), custom_call_target="tpu_custom_call" | custom-call | tf_op jit(solution)/shard_map/total_gradient/pallas_call | solution.py:117
  206.4 3.8 %renewed_block.1.h_ref = bf16[3,512,256]{2,1,0:T(8,128)(2,1)} custom-call(s32[4]{0:T(128)} %pad_add_fusion.pos, f32[3,512,256]{2,1,0:T(8,128)} %get-tuple-element.79.g_ref, bf16[3,512,256]{2,1,0:T(8,128)(2,1)} %get-tuple-element.80.w_ref, f32[8,512]{1,0:T(8,128)} %get-tuple-element.81.sq_ref, f32[8,128]{1,0:T(8,128)} %get-tuple-element.82.sums_ref, ...), custom_call_target="tpu_custom_call" | custom-call | tf_op jit(solution)/shard_map/renewed_block/pallas_call | solution.py:117
  214.1 31.8 %collective-permute-done.39.refs_1_.h_ref = bf16[3,512,256]{2,1,0:T(8,128)(2,1)} collective-permute-done((bf16[3,512,256]{2,1,0:T(8,128)(2,1)}, bf16[3,512,256]{2,1,0:T(8,128)(2,1)}, u32[]{:S(2)}, u32[]{:S(2)}) %collective-permute-start.39) | collective-permute-done | bytes 786464 | tf_op jit(solution)/shard_map/ppermute | solution.py:460
  247.4 7.7 %apply_renewed.4 = (bf16[8,1024,512]{2,1,0:T(8,128)(2,1)}, bf16[1024,512]{1,0:T(8,128)(2,1)}) custom-call(s32[4]{0:T(128)} %pad_add_fusion.pos, bf16[8,1024,512]{2,1,0:T(8,128)(2,1)} %q0.7, bf16[4,1024,512]{2,1,0:T(8,128)(2,1)} %collective-permute-done.7.q1, bf16[3,512,256]{2,1,0:T(8,128)(2,1)} %renewed_block.1.h_ref, ...), custom_call_target="tpu_custom_call" | custom-call | flops 3221225472 | bytes 7340032 | tf_op jit(solution)/shard_map/apply_renewed/pallas_call | solution.py:117
  255.2 10.4 %collective-permute-done.40.rest_0_.refs_1_.h_ref = bf16[3,512,256]{2,1,0:T(8,128)(2,1)} collective-permute-done((bf16[3,512,256]{2,1,0:T(8,128)(2,1)}, bf16[3,512,256]{2,1,0:T(8,128)(2,1)}, u32[]{:S(2)}, u32[]{:S(2)}) %collective-permute-start.40) | collective-permute-done | bytes 786464 | tf_op jit(solution)/shard_map/ppermute | solution.py:460
  270.2 7.4 %apply_renewed.5 = (bf16[8,1024,512]{2,1,0:T(8,128)(2,1)}, bf16[1024,512]{1,0:T(8,128)(2,1)}) custom-call(s32[4]{0:T(128)} %pad_add_fusion.pos, bf16[8,1024,512]{2,1,0:T(8,128)(2,1)} %q0.7, bf16[4,1024,512]{2,1,0:T(8,128)(2,1)} %collective-permute-done.7.q1, ...), custom_call_target="tpu_custom_call", output_to_operand_aliasing={{0}: (6, {})} | custom-call | flops 3221225472 | bytes 7340032 | tf_op jit(solution)/shard_map/apply_renewed/pallas_call | solution.py:117
  277.7 9.9 %collective-permute-done.43.refs_2_.s_ref = bf16[3,512,256]{2,1,0:T(8,128)(2,1)} collective-permute-done((bf16[3,512,256]{2,1,0:T(8,128)(2,1)}, bf16[3,512,256]{2,1,0:T(8,128)(2,1)}, u32[]{:S(2)}, u32[]{:S(2)}) %collective-permute-start.43) | collective-permute-done | bytes 786464 | tf_op jit(solution)/shard_map/ppermute | solution.py:457
  287.6 7.8 %apply_renewed.6 = (bf16[8,1024,512]{2,1,0:T(8,128)(2,1)}, bf16[1024,512]{1,0:T(8,128)(2,1)}) custom-call(s32[4]{0:T(128)} %pad_add_fusion.pos, bf16[8,1024,512]{2,1,0:T(8,128)(2,1)} %q0.7, bf16[4,1024,512]{2,1,0:T(8,128)(2,1)} %collective-permute-done.7.q1, ...), custom_call_target="tpu_custom_call", output_to_operand_aliasing={{0}: (8, {})} | custom-call | flops 3221225472 | bytes 7340032 | tf_op jit(solution)/shard_map/apply_renewed/pallas_call | solution.py:117
  295.4 7.8 %apply_renewed.7 = (bf16[8,1024,512]{2,1,0:T(8,128)(2,1)}, bf16[1024,512]{1,0:T(8,128)(2,1)}) custom-call(s32[4]{0:T(128)} %pad_add_fusion.pos, bf16[8,1024,512]{2,1,0:T(8,128)(2,1)} %q0.7, bf16[4,1024,512]{2,1,0:T(8,128)(2,1)} %collective-permute-done.7.q1, ...), custom_call_target="tpu_custom_call", output_to_operand_aliasing={{0}: (6, {})} | custom-call | flops 3221225472 | bytes 7340032 | tf_op jit(solution)/shard_map/apply_renewed/pallas_call | solution.py:117
  306.4 3.5 %place.1 = bf16[8,1024,512]{2,1,0:T(8,128)(2,1)} custom-call(s32[4]{0:T(128)} %pad_add_fusion.pos, bf16[1024,512]{1,0:T(8,128)(2,1)} %collective-permute-done.45.refs_0_, bf16[1024,512]{1,0:T(8,128)(2,1)} %collective-permute-done.47.refs_1_, bf16[8,1024,512]{2,1,0:T(8,128)(2,1)} %get-tuple-element.90.refs_2_), custom_call_target="tpu_custom_call", output_to_operand_aliasing={{}: (3, {})} | custom-call | bytes 3000000 | tf_op jit(solution)/shard_map/place/pallas_call | solution.py:117
  (105 shorter events, 96.5 us)
Async XLA Ops:
  0.0 73.8 %collective-permute-start.8 = (bf16[8,1024,512]{2,1,0:T(8,128)(2,1)}, bf16[8,1024,512]{2,1,0:T(8,128)(2,1)}, u32[]{:S(2)}, u32[]{:S(2)}) collective-permute-start(bf16[8,1024,512]{2,1,0:T(8,128)(2,1)} %k0.7), channel_id=1, source_target_pairs={{0,1},{1,0},{2,3},{3,2},{4,5},{5,4},{6,7},{7,6},{8,9},{9,8},{10,11... | collective-permute-start | bytes 25165832 | tf_op jit(solution)/shard_map/ppermute | solution.py:451
  0.5 75.3 %collective-permute-start.9 = (bf16[8,1024,512]{2,1,0:T(8,128)(2,1)}, bf16[8,1024,512]{2,1,0:T(8,128)(2,1)}, u32[]{:S(2)}, u32[]{:S(2)}) collective-permute-start(bf16[8,1024,512]{2,1,0:T(8,128)(2,1)} %v0.7), channel_id=1, source_target_pairs={{0,1},{1,0},{2,3},{3,2},{4,5},{5,4},{6,7},{7,6},{8,9},{9,8},{10,11... | collective-permute-start | bytes 25165832 | tf_op jit(solution)/shard_map/ppermute | solution.py:451
  36.5 24.1 %collective-permute-start.15 = (bf16[4,3,64,256]{3,2,1,0:T(8,128)(2,1)}, bf16[4,3,64,256]{3,2,1,0:T(8,128)(2,1)}, u32[]{:S(2)}, u32[]{:S(2)}) collective-permute-start(bf16[4,3,64,256]{3,2,1,0:T(8,128)(2,1)} %get-tuple-element.53.rest_0_.refs_6_), channel_id=1, source_target_pairs={{0,16},{16,0},{1,17},{17,1},{2,18},{18,2},{3,19},{19,3},{4,20},{20... | collective-permute-start | bytes 1179656 | tf_op jit(solution)/shard_map/ppermute | solution.py:454
  69.9 24.0 %collective-permute-start.20 = (bf16[4,3,128,256]{3,2,1,0:T(8,128)(2,1)}, bf16[4,3,128,256]{3,2,1,0:T(8,128)(2,1)}, u32[]{:S(2)}, u32[]{:S(2)}) collective-permute-start(bf16[4,3,128,256]{3,2,1,0:T(8,128)(2,1)} %get-tuple-element.62.rest_4_.rest_0_), channel_id=1, source_target_pairs={{0,16},{16,0},{1,17},{17,1},{2,18},{18,2},{3,19},{19,3},{4,20},{20... | collective-permute-start | bytes 2359304 | tf_op jit(solution)/shard_map/ppermute | solution.py:454
  71.3 20.0 %collective-permute-start.17 = (bf16[3,128,256]{2,1,0:T(8,128)(2,1)}, bf16[3,128,256]{2,1,0:T(8,128)(2,1)}, u32[]{:S(2)}, u32[]{:S(2)}) collective-permute-start(bf16[3,128,256]{2,1,0:T(8,128)(2,1)} %get-tuple-element.59), channel_id=1, source_target_pairs={{0,4},{2,6},{4,0},{6,2},{8,12},{10,14},{12,8},{14,10},{1,5},{3,7},... | collective-permute-start | bytes 589832 | tf_op jit(solution)/shard_map/ppermute | solution.py:460
  71.3 20.5 %collective-permute-start.18 = (bf16[3,128,256]{2,1,0:T(8,128)(2,1)}, bf16[3,128,256]{2,1,0:T(8,128)(2,1)}, u32[]{:S(2)}, u32[]{:S(2)}) collective-permute-start(bf16[3,128,256]{2,1,0:T(8,128)(2,1)} %get-tuple-element.60), channel_id=1, source_target_pairs={{0,8},{2,10},{4,12},{6,14},{8,0},{10,2},{12,4},{14,6},{1,9},{3,11}... | collective-permute-start | bytes 589832 | tf_op jit(solution)/shard_map/ppermute | solution.py:460
  73.8 19.5 %collective-permute-start.19 = (bf16[3,128,256]{2,1,0:T(8,128)(2,1)}, bf16[3,128,256]{2,1,0:T(8,128)(2,1)}, u32[]{:S(2)}, u32[]{:S(2)}) collective-permute-start(bf16[3,128,256]{2,1,0:T(8,128)(2,1)} %get-tuple-element.61), channel_id=1, source_target_pairs={{0,12},{2,14},{4,8},{6,10},{8,4},{10,6},{12,0},{14,2},{1,13},{3,15... | collective-permute-start | bytes 589832 | tf_op jit(solution)/shard_map/ppermute | solution.py:460
  97.2 30.2 %collective-permute-start.28 = (bf16[4,3,128,256]{3,2,1,0:T(8,128)(2,1)}, bf16[4,3,128,256]{3,2,1,0:T(8,128)(2,1)}, u32[]{:S(2)}, u32[]{:S(2)}) collective-permute-start(bf16[4,3,128,256]{3,2,1,0:T(8,128)(2,1)} %get-tuple-element.72.refs_4_.rest_0_), channel_id=1, source_target_pairs={{0,16},{16,0},{1,17},{17,1},{2,18},{18,2},{3,19},{19,3},{4,20},{20... | collective-permute-start | bytes 2359304 | tf_op jit(solution)/shard_map/ppermute | solution.py:454
  98.0 149.5 %collective-permute-start.7 = (bf16[4,1024,512]{2,1,0:T(8,128)(2,1)}, bf16[4,1024,512]{2,1,0:T(8,128)(2,1)}, u32[]{:S(2)}, u32[]{:S(2)}) collective-permute-start(bf16[4,1024,512]{2,1,0:T(8,128)(2,1)} %other_half.1.refs_10_), channel_id=1, source_target_pairs={{0,1},{1,0},{2,3},{3,2},{4,5},{5,4},{6,7},{7,6},{8,9},{9,8},{10,11... | collective-permute-start | bytes 12582920 | tf_op jit(solution)/shard_map/ppermute | solution.py:451
  102.2 23.6 %collective-permute-start.21 = (bf16[3,128,256]{2,1,0:T(8,128)(2,1)}, bf16[3,128,256]{2,1,0:T(8,128)(2,1)}, u32[]{:S(2)}, u32[]{:S(2)}) collective-permute-start(bf16[3,128,256]{2,1,0:T(8,128)(2,1)} %get-tuple-element.65), channel_id=1, source_target_pairs={{0,4},{2,6},{4,0},{6,2},{8,12},{10,14},{12,8},{14,10},{1,5},{3,7},... | collective-permute-start | bytes 589832 | tf_op jit(solution)/shard_map/ppermute | solution.py:460
  104.3 21.5 %collective-permute-start.22 = (bf16[3,128,256]{2,1,0:T(8,128)(2,1)}, bf16[3,128,256]{2,1,0:T(8,128)(2,1)}, u32[]{:S(2)}, u32[]{:S(2)}) collective-permute-start(bf16[3,128,256]{2,1,0:T(8,128)(2,1)} %get-tuple-element.66), channel_id=1, source_target_pairs={{0,8},{2,10},{4,12},{6,14},{8,0},{10,2},{12,4},{14,6},{1,9},{3,11}... | collective-permute-start | bytes 589832 | tf_op jit(solution)/shard_map/ppermute | solution.py:460
  106.4 20.9 %collective-permute-start.23 = (bf16[3,128,256]{2,1,0:T(8,128)(2,1)}, bf16[3,128,256]{2,1,0:T(8,128)(2,1)}, u32[]{:S(2)}, u32[]{:S(2)}) collective-permute-start(bf16[3,128,256]{2,1,0:T(8,128)(2,1)} %get-tuple-element.67), channel_id=1, source_target_pairs={{0,12},{2,14},{4,8},{6,10},{8,4},{10,6},{12,0},{14,2},{1,13},{3,15... | collective-permute-start | bytes 589832 | tf_op jit(solution)/shard_map/ppermute | solution.py:460
  125.7 19.7 %collective-permute-start.31 = (bf16[3,512,256]{2,1,0:T(8,128)(2,1)}, bf16[3,512,256]{2,1,0:T(8,128)(2,1)}, u32[]{:S(2)}, u32[]{:S(2)}) collective-permute-start(bf16[3,512,256]{2,1,0:T(8,128)(2,1)} %added.4.rest_2_), channel_id=1, source_target_pairs={{0,4},{2,6},{4,0},{6,2},{8,12},{10,14},{12,8},{14,10},{1,5},{3,7},... | collective-permute-start | bytes 2359304 | tf_op jit(solution)/shard_map/ppermute | solution.py:460
  125.8 19.6 %collective-permute-start.30 = (bf16[3,512,256]{2,1,0:T(8,128)(2,1)}, bf16[3,512,256]{2,1,0:T(8,128)(2,1)}, u32[]{:S(2)}, u32[]{:S(2)}) collective-permute-start(bf16[3,512,256]{2,1,0:T(8,128)(2,1)} %get-tuple-element.74), channel_id=1, source_target_pairs={{0,2},{2,0},{4,6},{6,4},{8,10},{10,8},{12,14},{14,12},{1,3},{3,1},... | collective-permute-start | bytes 2359304 | tf_op jit(solution)/shard_map/ppermute | solution.py:457
  144.9 22.6 %collective-permute-start.33 = (bf16[3,512,256]{2,1,0:T(8,128)(2,1)}, bf16[3,512,256]{2,1,0:T(8,128)(2,1)}, u32[]{:S(2)}, u32[]{:S(2)}) collective-permute-start(bf16[3,512,256]{2,1,0:T(8,128)(2,1)} %get-tuple-element.77), channel_id=1, source_target_pairs={{0,2},{2,0},{4,6},{6,4},{8,10},{10,8},{12,14},{14,12},{1,3},{3,1},... | collective-permute-start | bytes 2359304 | tf_op jit(solution)/shard_map/ppermute | solution.py:457
  149.0 32.5 %collective-permute-start.32 = (bf16[3,512,256]{2,1,0:T(8,128)(2,1)}, bf16[3,512,256]{2,1,0:T(8,128)(2,1)}, u32[]{:S(2)}, u32[]{:S(2)}) collective-permute-start(bf16[3,512,256]{2,1,0:T(8,128)(2,1)} %added.5.rest_2_), channel_id=1, source_target_pairs={{0,8},{2,10},{4,12},{6,14},{8,0},{10,2},{12,4},{14,6},{1,9},{3,11}... | collective-permute-start | bytes 2359304 | tf_op jit(solution)/shard_map/ppermute | solution.py:460
  165.9 19.2 %collective-permute-start.34 = (bf16[3,512,256]{2,1,0:T(8,128)(2,1)}, bf16[3,512,256]{2,1,0:T(8,128)(2,1)}, u32[]{:S(2)}, u32[]{:S(2)}) collective-permute-start(bf16[3,512,256]{2,1,0:T(8,128)(2,1)} %get-tuple-element.78), channel_id=1, source_target_pairs={{0,2},{2,0},{4,6},{6,4},{8,10},{10,8},{12,14},{14,12},{1,3},{3,1},... | collective-permute-start | bytes 2359304 | tf_op jit(solution)/shard_map/ppermute | solution.py:457
  170.7 27.6 %collective-permute-start.35 = (bf16[3,512,256]{2,1,0:T(8,128)(2,1)}, bf16[3,512,256]{2,1,0:T(8,128)(2,1)}, u32[]{:S(2)}, u32[]{:S(2)}) collective-permute-start(bf16[3,512,256]{2,1,0:T(8,128)(2,1)} %added.6.refs_1_), channel_id=1, source_target_pairs={{0,4},{2,6},{4,0},{6,2},{8,12},{10,14},{12,8},{14,10},{1,5},{3,7},... | collective-permute-start | bytes 2359304 | tf_op jit(solution)/shard_map/ppermute | solution.py:460
  210.2 35.7 %collective-permute-start.39 = (bf16[3,512,256]{2,1,0:T(8,128)(2,1)}, bf16[3,512,256]{2,1,0:T(8,128)(2,1)}, u32[]{:S(2)}, u32[]{:S(2)}) collective-permute-start(bf16[3,512,256]{2,1,0:T(8,128)(2,1)} %renewed_block.1.h_ref), channel_id=1, source_target_pairs={{0,8},{2,10},{4,12},{6,14},{8,0},{10,2},{12,4},{14,6},{1,9},{3,11}... | collective-permute-start | bytes 2359304 | tf_op jit(solution)/shard_map/ppermute | solution.py:460
  210.2 37.3 %collective-permute-start.38 = (bf16[3,512,256]{2,1,0:T(8,128)(2,1)}, bf16[3,512,256]{2,1,0:T(8,128)(2,1)}, u32[]{:S(2)}, u32[]{:S(2)}) collective-permute-start(bf16[3,512,256]{2,1,0:T(8,128)(2,1)} %renewed_block.1.h_ref), channel_id=1, source_target_pairs={{0,2},{2,0},{4,6},{6,4},{8,10},{10,8},{12,14},{14,12},{1,3},{3,1},... | collective-permute-start | bytes 2359304 | tf_op jit(solution)/shard_map/ppermute | solution.py:457
  211.7 35.8 %collective-permute-start.37 = (bf16[3,512,256]{2,1,0:T(8,128)(2,1)}, bf16[3,512,256]{2,1,0:T(8,128)(2,1)}, u32[]{:S(2)}, u32[]{:S(2)}) collective-permute-start(bf16[3,512,256]{2,1,0:T(8,128)(2,1)} %renewed_block.1.h_ref), channel_id=1, source_target_pairs={{0,4},{2,6},{4,0},{6,2},{8,12},{10,14},{12,8},{14,10},{1,5},{3,7},... | collective-permute-start | bytes 2359304 | tf_op jit(solution)/shard_map/ppermute | solution.py:460
  245.9 19.7 %collective-permute-start.40 = (bf16[3,512,256]{2,1,0:T(8,128)(2,1)}, bf16[3,512,256]{2,1,0:T(8,128)(2,1)}, u32[]{:S(2)}, u32[]{:S(2)}) collective-permute-start(bf16[3,512,256]{2,1,0:T(8,128)(2,1)} %collective-permute-done.39.refs_1_.h_ref), channel_id=1, source_target_pairs={{0,4},{2,6},{4,0},{6,2},{8,12},{10,14},{12,8},{14,10},{1,5},{3,7},... | collective-permute-start | bytes 2359304 | tf_op jit(solution)/shard_map/ppermute | solution.py:460
  245.9 24.2 %collective-permute-start.44 = (bf16[3,512,256]{2,1,0:T(8,128)(2,1)}, bf16[3,512,256]{2,1,0:T(8,128)(2,1)}, u32[]{:S(2)}, u32[]{:S(2)}) collective-permute-start(bf16[3,512,256]{2,1,0:T(8,128)(2,1)} %collective-permute-done.39.refs_1_.h_ref), channel_id=1, source_target_pairs={{0,2},{2,0},{4,6},{6,4},{8,10},{10,8},{12,14},{14,12},{1,3},{3,1},... | collective-permute-start | bytes 2359304 | tf_op jit(solution)/shard_map/ppermute | solution.py:457
  255.1 22.6 %collective-permute-start.42 = (bf16[1024,512]{1,0:T(8,128)(2,1)}, bf16[1024,512]{1,0:T(8,128)(2,1)}, u32[]{:S(2)}, u32[]{:S(2)}) collective-permute-start(bf16[1024,512]{1,0:T(8,128)(2,1)} %get-tuple-element.84), channel_id=1, source_target_pairs={{0,1},{1,0},{2,3},{3,2},{4,5},{5,4},{6,7},{7,6},{8,9},{9,8},{10,11... | collective-permute-start | bytes 3145736 | tf_op jit(solution)/shard_map/ppermute | solution.py:451
  (27 other events, 255.5 us)
